TPU v7x, 256 devices: a whole 4x4x8 slice. The times are simulated.
256 devices in a mesh: leaf: 64 (over z, x, core), near: 4 (over y).
Axes of the slice: x: 4, y: 4, z: 8, core: 2. Of those that a mesh axis runs over, the one named last changes fastest.
Arguments:
- vectors: bfloat16 [256, 131072], P(None, 'leaf'), may hold values from -6 to 6
- near_blocks: bfloat16 [512, 32, 256, 256], P('leaf', 'near'), may hold values from -0.0625 to 0.0625
- near_cols: int32 [512, 32], P('leaf', 'near'), may hold values from 0 to 511, as said below
- near_count: int32 [512], P('leaf'), may hold values from 8 to 32, as said below
- col_basis: bfloat16 [64, 131072], P(None, 'leaf'), may hold values from -0.375 to 0.375
- row_basis: bfloat16 [64, 131072], P(None, 'leaf'), may hold values from -0.1875 to 0.1875
- local_transfer: bfloat16 [448, 64, 128], P('leaf'), may hold values from -0.5 to 0.5
- local_coupling: bfloat16 [960, 64, 512], P('leaf', None, 'near'), may hold values from -0.25 to 0.25
- local_partners: int32 [960, 8], P('leaf', 'near'), may hold values from 0 to 511, as said below
- upper_transfer: bfloat16 [63, 64, 128], replicated, may hold values from -0.5 to 0.5
- upper_coupling: bfloat16 [63, 64, 512], P(None, None, 'near'), may hold values from -0.25 to 0.25
- upper_partners: int32 [63, 8], P(None, 'near'), may hold values from 0 to 31
Outputs:
- result: bfloat16 [256, 131072], P('near', 'leaf')
Inputs may be any that keep to these rules, and one draw needn't show every extreme that they name: `near_cols`: slot 0 of every leaf row names that leaf; every entry names a leaf at most 8 away. `near_count`: some leaf row has all 32 slots live. `local_partners`: a node of level k names nodes of level k at most 8 / 2**k away.
All inputs are finite; a program needn't handle non-finite values.
Results may differ from a plain program's by a relative error of at most 0.004.
Values may be sent and summed in bfloat16 or wider, within the bound.
A program may use at most 128 MiB of HBM per device.

v0:
```python
import jax
import jax.numpy as jnp
from jax import lax
from jax.sharding import PartitionSpec as P


def extended(value, sides, width):
    for axis, dim in sides:
        size, length = (lax.axis_size(axis), value.shape[dim])
        up = [(i, (i + 1) % size) for i in range(size - 1)]
        down = [(j, i) for i, j in up]
        last = lax.slice_in_dim(value, length - width, length, axis=dim)
        initial = lax.slice_in_dim(value, 0, width, axis=dim)
        before = lax.ppermute(last, axis, up)
        after = lax.ppermute(initial, axis, down)
        value = jnp.concatenate([before, value, after], axis=dim)
    return value


def gather_pieces(source, picks, nodes):
    taken = jnp.take(source, picks.reshape(-1), axis=0)
    return taken.reshape(nodes, -1, source.shape[2])


def descend(
    local_sum,
    upper_sum,
    ups,
    offsets,
    upper_transfer,
    row_basis,
    leaf_index,
    leaf_width,
    leaf_dev,
    width,
    rank,
):
    highest = lax.Precision.HIGHEST
    span = local_sum.shape[2]
    levels_upper = len(offsets)
    field = upper_sum[offsets[-1] : offsets[-1] + 1]
    for level in range(levels_upper - 1, -1, -1):
        half = leaf_width >> level + 1
        begin = offsets[level]
        mats = upper_transfer[begin : begin + half].astype(jnp.float32)
        down = jnp.einsum("pba,pbc->pac", mats, field, precision=highest)
        down = down.reshape(2 * half, rank, span)
        if level > 0:
            lower = offsets[level - 1]
            field = upper_sum[lower : lower + 2 * half] + down
        else:
            field = lax.dynamic_slice_in_dim(down, leaf_index, 1, 0)
    top = 2 * leaf_dev - 2
    field = field + local_sum[top : top + 1]
    count = 1
    for level in range(len(ups) - 1, -1, -1):
        down = jnp.einsum("pba,pbc->pac", ups[level].astype(jnp.float32), field, precision=highest)
        down = down.reshape(2 * count, rank, span)
        count = count * 2
        start = 2 * leaf_dev - 2 * count
        field = local_sum[start : start + count] + down
    row_leaves = row_basis.reshape(rank, leaf_dev, width).astype(jnp.float32)
    far = jnp.einsum("iac,ail->cil", field, row_leaves, precision=highest)
    return far.reshape(span, leaf_dev * width)


def local(
    vectors,
    near_blocks,
    near_cols,
    near_count,
    col_basis,
    row_basis,
    local_transfer,
    local_coupling,
    local_partners,
    upper_transfer,
    upper_coupling,
    upper_partners,
):
    leaf_index = lax.axis_index("leaf")
    near_index = lax.axis_index("near")
    leaf_width = lax.axis_size("leaf")
    leaf_dev = near_blocks.shape[0]
    slot_dev = near_blocks.shape[1]
    width = near_blocks.shape[2]
    rank = col_basis.shape[0]
    cols = vectors.shape[0]
    wide = extended(vectors, (("leaf", 1),), leaf_dev * width)
    wide_leaves = wide.reshape(cols, 3 * leaf_dev, width)
    local_cols = near_cols - (leaf_index - 1) * leaf_dev
    picked = jnp.take(wide_leaves, local_cols.reshape(-1), axis=1).reshape(
        cols, leaf_dev, slot_dev, width
    )
    slot_ids = near_index * slot_dev + jnp.arange(slot_dev, dtype=jnp.int32)
    live = slot_ids[None, :] < near_count[:, None]
    picked = jnp.where(live[None, :, :, None], picked, jnp.zeros_like(picked))
    near_terms = jnp.einsum(
        "cisa,isab->cib", picked, near_blocks, preferred_element_type=jnp.float32
    )
    near_terms = near_terms.reshape(cols, leaf_dev * width)
    leaf_vectors = vectors.reshape(cols, leaf_dev, width)
    basis = col_basis.reshape(rank, leaf_dev, width)
    coef = jnp.einsum(
        "ail,cil->iac", basis, leaf_vectors, preferred_element_type=jnp.float32
    ).astype(jnp.bfloat16)
    levels_local = leaf_dev.bit_length() - 1
    coefs = [coef]
    ups = []
    fields = []
    count = leaf_dev
    for level in range(levels_local + 1):
        start = 2 * leaf_dev - 2 * count
        rim = extended(coefs[-1], (("leaf", 0),), count)
        picks = local_partners[start : start + count] - (leaf_index - 1) * count
        stacked = gather_pieces(rim, picks, count)
        fields.append(
            jnp.einsum(
                "nab,nbc->nac",
                local_coupling[start : start + count],
                stacked,
                preferred_element_type=jnp.float32,
            )
        )
        if level < levels_local:
            half = count // 2
            pstart = leaf_dev - 2 * half
            emats = local_transfer[pstart : pstart + half]
            ups.append(emats)
            pairs = coefs[-1].reshape(half, 2 * rank, cols)
            coefs.append(
                jnp.einsum("pab,pbc->pac", emats, pairs, preferred_element_type=jnp.float32).astype(
                    jnp.bfloat16
                )
            )
            count = half
    summit = lax.all_gather(coefs[-1], "leaf", axis=0, tiled=True)
    levels_upper = leaf_width.bit_length() - 1
    upper_coefs = [summit]
    offsets = []
    count = leaf_width
    start = 0
    for level in range(levels_upper):
        half = count // 2
        offsets.append(start)
        pairs = upper_coefs[-1].reshape(half, 2 * rank, cols)
        upper_coefs.append(
            jnp.einsum(
                "pab,pbc->pac",
                upper_transfer[start : start + half],
                pairs,
                preferred_element_type=jnp.float32,
            ).astype(jnp.bfloat16)
        )
        start = start + half
        count = half
    upper_parts = []
    for level in range(levels_upper):
        half = leaf_width >> level + 1
        begin = offsets[level]
        stacked = gather_pieces(upper_coefs[level + 1], upper_partners[begin : begin + half], half)
        upper_parts.append(
            jnp.einsum(
                "nab,nbc->nac",
                upper_coupling[begin : begin + half],
                stacked,
                preferred_element_type=jnp.float32,
            )
        )
    local_full = jnp.concatenate(fields, axis=0)
    upper_full = jnp.concatenate(upper_parts, axis=0)
    near_share = lax.psum_scatter(near_terms, "near", scatter_dimension=0, tiled=True)
    local_sum, upper_sum = (
        lax.psum_scatter(local_full, "near", scatter_dimension=2, tiled=True),
        lax.psum_scatter(upper_full, "near", scatter_dimension=2, tiled=True),
    )
    far = descend(
        local_sum,
        upper_sum,
        ups,
        offsets,
        upper_transfer,
        row_basis,
        leaf_index,
        leaf_width,
        leaf_dev,
        width,
        rank,
    )
    return (near_share + far).astype(jnp.bfloat16)


def solution(mesh):
    return jax.shard_map(
        local,
        mesh=mesh,
        in_specs=(
            P(None, "leaf"),
            P("leaf", "near", None, None),
            P("leaf", "near"),
            P("leaf"),
            P(None, "leaf"),
            P(None, "leaf"),
            P("leaf", None, None),
            P("leaf", None, "near"),
            P("leaf", "near"),
            P(),
            P(None, None, "near"),
            P(None, "near"),
        ),
        out_specs=P("near", "leaf"),
        check_vma=False,
    )
```

profile of v0, /device:TPU:1, one launch (start us, length us, event | category | flops | bytes accessed | tf_op | source)
XLA Modules:
  0.0 233.6 jit_solution(1660197679456511118)
XLA Ops:
  7.4 1.8 convolution_convert_fusion.3
  9.2 1.0 convolution_convert_fusion.5
  10.2 0.9 convolution_convert_fusion.7
  11.1 0.9 convolution_convert_fusion.9
  11.9 4.5 %collective-permute-start.8 = (bf16[1,64,256]{2,1,0:T(8,128)(2,1)S(1)}, bf16[1,64,256]{2,1,0:T(8,128)(2,1)S(1)}, u32[]{:S(2)}, u32[]{:S(2)}) collective-permute-start(bf16[1,64,256]{2,1,0:T(8,128)(2,1)S(1)} %bitcast.274), channel_id=1, source_target_pairs={{0,4},{4,8},{8,12},{12,16},{16,20},{20,24},{24,28},{28,32},{32,36}... | collective-permute-start | bytes 98312 | tf_op jit(solution)/shard_map/ppermute | solution.py:14
  16.5 1.9 collective-permute-start.9
  18.4 3.6 %collective-permute-start.6 = (bf16[2,64,256]{2,1,0:T(8,128)(2,1)S(1)}, bf16[2,64,256]{2,1,0:T(8,128)(2,1)S(1)}, u32[]{:S(2)}, u32[]{:S(2)}) collective-permute-start(bf16[2,64,256]{2,1,0:T(8,128)(2,1)S(1)} %bitcast.269), channel_id=1, source_target_pairs={{0,4},{4,8},{8,12},{12,16},{16,20},{20,24},{24,28},{28,32},{32,36}... | collective-permute-start | bytes 196616 | tf_op jit(solution)/shard_map/ppermute | solution.py:14
  22.0 1.9 collective-permute-start.7
  24.1 3.6 %collective-permute-start.4 = (bf16[4,64,256]{2,1,0:T(8,128)(2,1)S(1)}, bf16[4,64,256]{2,1,0:T(8,128)(2,1)S(1)}, u32[]{:S(2)}, u32[]{:S(2)}) collective-permute-start(bf16[4,64,256]{2,1,0:T(8,128)(2,1)S(1)} %bitcast.259), channel_id=1, source_target_pairs={{0,4},{4,8},{8,12},{12,16},{16,20},{20,24},{24,28},{28,32},{32,36}... | collective-permute-start | bytes 393224 | tf_op jit(solution)/shard_map/ppermute | solution.py:14
  30.7 0.9 subtract_reduce_fusion
  33.1 0.8 copy.190
  34.7 0.8 compare_and_fusion.8
  35.6 0.8 compare_and_fusion.9
  36.6 0.9 slice_reduce_fusion
  43.6 1.9 collective-permute-start.5
  45.5 3.6 %collective-permute-start.2 = (bf16[8,64,256]{2,1,0:T(8,128)(2,1)S(1)}, bf16[8,64,256]{2,1,0:T(8,128)(2,1)S(1)}, u32[]{:S(2)}, u32[]{:S(2)}) collective-permute-start(bf16[8,64,256]{2,1,0:T(8,128)(2,1)S(1)} %convolution_convert_fusion.3), channel_id=1, source_target_pairs={{0,4},{4,8},{8,12},{12,16},{16,20},{20,24},{24,28},{28,32},{32,36}... | collective-permute-start | bytes 786440 | tf_op jit(solution)/shard_map/ppermute | solution.py:14
  49.2 0.8 pad_maximum_fusion.5
  50.6 0.8 convolution_bitcast_fusion.14
  51.5 1.9 collective-permute-start.3
  55.2 4.4 %collective-permute-done.3 = bf16[8,64,256]{2,1,0:T(8,128)(2,1)S(1)} collective-permute-done((bf16[8,64,256]{2,1,0:T(8,128)(2,1)S(1)}, bf16[8,64,256]{2,1,0:T(8,128)(2,1)S(1)}, u32[]{:S(2)}, u32[]{:S(2)}) %collective-permute-start.3) | collective-permute-done | bytes 262176 | tf_op jit(solution)/shard_map/ppermute | solution.py:15
  60.7 1.0 pad_maximum_fusion.1
  61.7 2.6 %copy.225 = f32[15,64,256]{1,0,2:T(8,128)S(1)} copy(f32[15,64,256]{2,1,0:T(8,128)} %pad_maximum_fusion.1) | data formatting | bytes 1966080
  64.3 1.6 reshape.790
  66.0 42.9 %all-gather.3.cloned.1.call-done = bf16[4096,256]{1,0:T(8,128)(2,1)} async-done(((bf16[64,256]{1,0:T(8,128)(2,1)}), bf16[4096,256]{1,0:T(8,128)(2,1)}) %all-gather.3.cloned.1.call-update) | async-done | bytes 2097168 | tf_op jit(solution)/shard_map/all_gather | solution.py:137
  108.9 2.0 convolution_convert_fusion
  112.6 1.2 bitcast_select_fusion.1
  114.4 1.0 bitcast_select_fusion.2
  116.0 0.8 bitcast_select_fusion.4
  118.3 0.8 bitcast_select_fusion
  119.5 1.8 bitcast_dynamic-update-slice_fusion
  121.3 1.3 fusion.7
  122.6 1.0 fusion.8
  123.6 0.9 fusion.9
  124.5 0.8 fusion.10
  125.3 0.8 fusion.11
  126.1 9.1 %copy.227 = f32[63,64,256]{1,0,2:T(8,128)} copy(f32[63,64,256]{2,1,0:T(8,128)} %fusion.11) | data formatting | bytes 8257536
  135.2 7.9 %reshape.792 = f32[256,4032]{1,0:T(8,128)} reshape(f32[256,63,64]{2,1,0:T(8,128)} %bitcast.229) | data formatting | bytes 8257536
  143.2 1.1 copy-done.5
  144.9 2.3 collective-permute-start
  147.2 2.2 collective-permute-start.1
  150.4 8.5 %collective-permute-done = bf16[256,2048]{0,1:T(8,128)(2,1)S(1)} collective-permute-done((bf16[256,2048]{0,1:T(8,128)(2,1)S(1)}, bf16[256,2048]{0,1:T(8,128)(2,1)S(1)}, u32[]{:S(2)}, u32[]{:S(2)}) %collective-permute-start) | collective-permute-done | bytes 1048608 | tf_op jit(solution)/shard_map/ppermute | solution.py:14
  158.9 4.8 %collective-permute-done.1 = bf16[256,2048]{0,1:T(8,128)(2,1)S(1)} collective-permute-done((bf16[256,2048]{0,1:T(8,128)(2,1)S(1)}, bf16[256,2048]{0,1:T(8,128)(2,1)S(1)}, u32[]{:S(2)}, u32[]{:S(2)}) %collective-permute-start.1) | collective-permute-done | bytes 1048608 | tf_op jit(solution)/shard_map/ppermute | solution.py:15
  163.7 1.8 pad_maximum_fusion
  165.5 3.2 %copy.175 = bf16[256,24,256]{2,0,1:T(8,128)(2,1)S(1)} copy(bf16[256,24,256]{0,2,1:T(8,128)(2,1)} %bitcast.232) | data formatting | bytes 6291456 | tf_op jit(solution)/shard_map/reshape | solution.py:90
  168.7 5.7 %gather_fusion = bf16[64,256,256]{2,1,0:T(8,128)(2,1)} fusion(bf16[256,24,256]{2,0,1:T(8,128)(2,1)S(1)} %copy.175, s32[1024]{0:T(1024)S(1)} %get-tuple-element.18), kind=kCustom, calls=%fused_computation | custom fusion | bytes 16777472 | tf_op jit(solution)/shard_map/jit(_take)/gather | solution.py:92
  174.4 9.0 %fusion = f32[8,256,256,1]{1,2,3,0:T(8,128)S(1)} fusion(bf16[8,8,256,256]{3,2,1,0:T(8,128)(2,1)} %param.13, bf16[256,8,8,256]{3,0,2,1:T(8,128)(2,1)} %bitcast.233, pred[8,8]{1,0:T(8,128)(4,1)S(1)} %get-tuple-element.11, pred[8,8]{1,0:T(8,128)(4,1)S(1)} %broadcast_compare_fusion), kind=kOutput, calls=%fused_computation.10 | convolution fusion | flops 2155872256 | bytes 18874496 | tf_op jit(solution)/shard_map/cisa,isab->cib/dot_general | solution.py:98
  183.4 1.8 copy.177
  185.4 1.1 reshape.791
  186.6 0.8 copy-done.3
  187.4 2.4 %reduce-scatter.12.cloned.1.call-done = f32[64,4032]{1,0:T(8,128)} async-done(((f32[256,4032]{1,0:T(8,128)}), f32[64,4032]{1,0:T(8,128)}) %reduce-scatter.12.cloned.1.call-update) | async-done | bytes 1032208
  189.9 2.3 reshape.793
  192.5 0.9 convolution_bitcast_fusion.17
  193.7 1.0 convolution_bitcast_fusion.12
  195.0 1.2 convolution_bitcast_fusion.6
  196.6 1.5 convolution_bitcast_fusion.5
  198.1 1.1 copy.212
  199.2 1.2 reshape.696
  200.7 2.3 convolution_bitcast_fusion.1
  203.9 1.0 slice_add_fusion.6
  205.5 1.0 slice_add_fusion.5
  207.0 1.0 slice_add_fusion.3
  207.9 1.3 convolution_bitcast_fusion.4
  209.3 14.9 %reduce-scatter.8.cloned.1.call-done = f32[64,2048]{1,0:T(8,128)} async-done(((f32[256,2048]{1,0:T(8,128)}), f32[64,2048]{1,0:T(8,128)}) %reduce-scatter.8.cloned.1.call-update) | async-done | bytes 524304 | tf_op jit(solution)/shard_map/reduce_scatter | solution.py:172
  224.2 1.8 add_convert_fusion
  (163 shorter events, 25.0 us)
Async XLA Ops:
  7.4 46.7 %copy-start.9 = (bf16[15,64,128]{2,1,0:T(8,128)(2,1)S(1)}, bf16[15,64,128]{2,1,0:T(8,128)(2,1)}, u32[]{:S(2)}) copy-start(bf16[15,64,128]{2,1,0:T(8,128)(2,1)} %param.19) | copy-start | bytes 737284
  7.4 101.5 %all-gather.3.cloned.1.call-start = ((), (), s32[]{:S(2)}) async-start(), calls=%async_computation.4 | async-start | bytes 2129920 | tf_op jit(solution)/shard_map/all_gather | solution.py:137
  11.9 12.0 %copy-start.8 = (bf16[256,64]{0,1:T(8,128)(2,1)}, bf16[256,64]{0,1:T(8,128)(2,1)S(1)}, u32[]{:S(2)}) copy-start(bf16[256,64]{0,1:T(8,128)(2,1)S(1)} %convolution_convert_fusion.9) | copy-start | bytes 98308
  11.9 31.7 %collective-permute-start.8 = (bf16[1,64,256]{2,1,0:T(8,128)(2,1)S(1)}, bf16[1,64,256]{2,1,0:T(8,128)(2,1)S(1)}, u32[]{:S(2)}, u32[]{:S(2)}) collective-permute-start(bf16[1,64,256]{2,1,0:T(8,128)(2,1)S(1)} %bitcast.274), channel_id=1, source_target_pairs={{0,4},{4,8},{8,12},{12,16},{16,20},{20,24},{24,28},{28,32},{32,36}... | collective-permute-start | bytes 98312 | tf_op jit(solution)/shard_map/ppermute | solution.py:14
  16.5 29.1 %collective-permute-start.9 = (bf16[1,64,256]{2,1,0:T(8,128)(2,1)S(1)}, bf16[1,64,256]{2,1,0:T(8,128)(2,1)S(1)}, u32[]{:S(2)}, u32[]{:S(2)}) collective-permute-start(bf16[1,64,256]{2,1,0:T(8,128)(2,1)S(1)} %bitcast.275), channel_id=1, source_target_pairs={{4,0},{8,4},{12,8},{16,12},{20,16},{24,20},{28,24},{32,28},{36,32}... | collective-permute-start | bytes 98312 | tf_op jit(solution)/shard_map/ppermute | solution.py:15
  18.4 33.1 %collective-permute-start.6 = (bf16[2,64,256]{2,1,0:T(8,128)(2,1)S(1)}, bf16[2,64,256]{2,1,0:T(8,128)(2,1)S(1)}, u32[]{:S(2)}, u32[]{:S(2)}) collective-permute-start(bf16[2,64,256]{2,1,0:T(8,128)(2,1)S(1)} %bitcast.269), channel_id=1, source_target_pairs={{0,4},{4,8},{8,12},{12,16},{16,20},{20,24},{24,28},{28,32},{32,36}... | collective-permute-start | bytes 196616 | tf_op jit(solution)/shard_map/ppermute | solution.py:14
  22.0 31.3 %collective-permute-start.7 = (bf16[2,64,256]{2,1,0:T(8,128)(2,1)S(1)}, bf16[2,64,256]{2,1,0:T(8,128)(2,1)S(1)}, u32[]{:S(2)}, u32[]{:S(2)}) collective-permute-start(bf16[2,64,256]{2,1,0:T(8,128)(2,1)S(1)} %bitcast.270), channel_id=1, source_target_pairs={{4,0},{8,4},{12,8},{16,12},{20,16},{24,20},{28,24},{32,28},{36,32}... | collective-permute-start | bytes 196616 | tf_op jit(solution)/shard_map/ppermute | solution.py:15
  24.0 161.4 %reduce-scatter.10.cloned.1.call-start = ((), (), s32[]{:S(2)}) async-start(), calls=%async_computation.5 | async-start | bytes 1310720
  24.1 30.2 %collective-permute-start.4 = (bf16[4,64,256]{2,1,0:T(8,128)(2,1)S(1)}, bf16[4,64,256]{2,1,0:T(8,128)(2,1)S(1)}, u32[]{:S(2)}, u32[]{:S(2)}) collective-permute-start(bf16[4,64,256]{2,1,0:T(8,128)(2,1)S(1)} %bitcast.259), channel_id=1, source_target_pairs={{0,4},{4,8},{8,12},{12,16},{16,20},{20,24},{24,28},{28,32},{32,36}... | collective-permute-start | bytes 393224 | tf_op jit(solution)/shard_map/ppermute | solution.py:14
  43.6 10.7 %collective-permute-start.5 = (bf16[4,64,256]{2,1,0:T(8,128)(2,1)S(1)}, bf16[4,64,256]{2,1,0:T(8,128)(2,1)S(1)}, u32[]{:S(2)}, u32[]{:S(2)}) collective-permute-start(bf16[4,64,256]{2,1,0:T(8,128)(2,1)S(1)} %bitcast.260), channel_id=1, source_target_pairs={{4,0},{8,4},{12,8},{16,12},{20,16},{24,20},{28,24},{32,28},{36,32}... | collective-permute-start | bytes 393224 | tf_op jit(solution)/shard_map/ppermute | solution.py:15
  45.5 9.7 %collective-permute-start.2 = (bf16[8,64,256]{2,1,0:T(8,128)(2,1)S(1)}, bf16[8,64,256]{2,1,0:T(8,128)(2,1)S(1)}, u32[]{:S(2)}, u32[]{:S(2)}) collective-permute-start(bf16[8,64,256]{2,1,0:T(8,128)(2,1)S(1)} %convolution_convert_fusion.3), channel_id=1, source_target_pairs={{0,4},{4,8},{8,12},{12,16},{16,20},{20,24},{24,28},{28,32},{32,36}... | collective-permute-start | bytes 786440 | tf_op jit(solution)/shard_map/ppermute | solution.py:14
  51.5 8.2 %collective-permute-start.3 = (bf16[8,64,256]{2,1,0:T(8,128)(2,1)S(1)}, bf16[8,64,256]{2,1,0:T(8,128)(2,1)S(1)}, u32[]{:S(2)}, u32[]{:S(2)}) collective-permute-start(bf16[8,64,256]{2,1,0:T(8,128)(2,1)S(1)} %convolution_convert_fusion.3), channel_id=1, source_target_pairs={{4,0},{8,4},{12,8},{16,12},{20,16},{24,20},{28,24},{32,28},{36,32}... | collective-permute-start | bytes 786440 | tf_op jit(solution)/shard_map/ppermute | solution.py:15
  61.7 47.2 %copy-start.1 = (bf16[63,64,128]{2,1,0:T(8,128)(2,1)S(1)}, bf16[63,64,128]{2,1,0:T(8,128)(2,1)}, u32[]{:S(2)}) copy-start(bf16[63,64,128]{2,1,0:T(8,128)(2,1)} %param.21) | copy-start | bytes 3096580
  66.0 123.9 %reduce-scatter.12.cloned.1.call-start = ((), (), s32[]{:S(2)}) async-start(), calls=%async_computation.6 | async-start | bytes 5242880
  118.2 1.2 copy-start.6
  118.3 3.1 %copy-start = (bf16[16,128,256]{2,1,0:T(8,128)(2,1)S(1)}, bf16[16,128,256]{2,1,0:T(8,128)(2,1)}, u32[]{:S(2)}) copy-start(bf16[16,128,256]{2,1,0:T(8,128)(2,1)} %bitcast_select_fusion.1) | copy-start | bytes 3145732
  119.5 3.2 %copy-start.2 = (bf16[8,128,256]{2,1,0:T(8,128)(2,1)S(1)}, bf16[8,128,256]{2,1,0:T(8,128)(2,1)}, u32[]{:S(2)}) copy-start(bf16[8,128,256]{2,1,0:T(8,128)(2,1)} %bitcast_select_fusion.2) | copy-start | bytes 1572868
  119.5 4.2 %copy-start.4 = (bf16[4,128,256]{2,1,0:T(8,128)(2,1)S(1)}, bf16[4,128,256]{2,1,0:T(8,128)(2,1)}, u32[]{:S(2)}) copy-start(bf16[4,128,256]{2,1,0:T(8,128)(2,1)} %bitcast_select_fusion.4) | copy-start | bytes 786436
  143.1 1.2 copy-start.5
  143.1 7.2 %copy-start.10 = (s32[8]{0:T(128)S(1)}, s32[8]{0:T(128)}, u32[]{:S(2)}) copy-start(s32[8]{0:T(128)} %param.15) | copy-start | bytes 100
  143.2 81.0 %reduce-scatter.8.cloned.1.call-start = ((), (), s32[]{:S(2)}) async-start(), calls=%async_computation.3 | async-start | bytes 2621440 | tf_op jit(solution)/shard_map/reduce_scatter | solution.py:172
  144.9 14.1 %collective-permute-start = (bf16[256,2048]{0,1:T(8,128)(2,1)S(1)}, bf16[256,2048]{0,1:T(8,128)(2,1)S(1)}, u32[]{:S(2)}, u32[]{:S(2)}) collective-permute-start(bf16[256,2048]{0,1:T(8,128)(2,1)S(1)} %copy.172), channel_id=1, source_target_pairs={{0,4},{4,8},{8,12},{12,16},{16,20},{20,24},{24,28},{28,32},{32,36}... | collective-permute-start | bytes 3145736 | tf_op jit(solution)/shard_map/ppermute | solution.py:14
  147.2 16.5 %collective-permute-start.1 = (bf16[256,2048]{0,1:T(8,128)(2,1)S(1)}, bf16[256,2048]{0,1:T(8,128)(2,1)S(1)}, u32[]{:S(2)}, u32[]{:S(2)}) collective-permute-start(bf16[256,2048]{0,1:T(8,128)(2,1)S(1)} %copy.172), channel_id=1, source_target_pairs={{4,0},{8,4},{12,8},{16,12},{20,16},{24,20},{28,24},{32,28},{36,32}... | collective-permute-start | bytes 3145736 | tf_op jit(solution)/shard_map/ppermute | solution.py:15
  183.4 1.9 copy-start.7
  186.5 0.9 copy-start.3
Sparse Core Ops, SparseCore 0:
  24.1 84.7 all-gather.2
Sparse Core Ops, SparseCore 1:
  66.0 38.3 reduce-scatter.9
  143.2 46.6 reduce-scatter.11
  192.3 31.8 reduce-scatter.7
where the time goes:
time: 235 us; the launch traced here: 234 us
  waiting for transfers between devices  78 us (33%)
  local copies, waits for them, and re-layouts  57.2 us (24%)
  matrix products  33.5 us (14%)
  starting transfers between devices  27.8 us (12%)
  other arithmetic  21.2 us (9%)
  between operations  15.8 us (7%)
    all_gather x1, waiting for transfers between devices, local(): summit = lax.all_gather(coefs[-1], 'leaf', axis=0, tiled=True)  42.9 us
    unnamed x29, local copies, waits for them, and re-layouts  27.5 us
    ppermute x5, starting transfers between devices, extended(): before = lax.ppermute(last, axis, up)  17.8 us
    reduce_scatter x1, waiting for transfers between devices, local(): lax.psum_scatter(near_terms, 'near', scatter_dimension=0, tiled=True)  14.9 us
    ppermute x5, starting transfers between devices, extended(): after = lax.ppermute(initial, axis, down)  9.92 us
    ppermute x5, waiting for transfers between devices, extended(): after = lax.ppermute(initial, axis, down)  9.18 us
    dot_general x1, matrix products, local(): jnp.einsum('cisa,isab->cib', picked, near_blocks, preferred_element_type=...  9 us
    ppermute x5, waiting for transfers between devices, extended(): before = lax.ppermute(last, axis, up)  8.55 us
  transfers between devices with their start and end apart: 14, of which 6 were waited for; matrix products, arithmetic and copies ran while one was open for 44% of the time, Pallas kernels for 0%

commit v1 on v0

v1 whole, which is shorter than its diff:
```python
import functools

import jax
import jax.numpy as jnp
from jax import lax
from jax.experimental import pallas as pl
from jax.experimental.pallas import tpu as pltpu
from jax.sharding import PartitionSpec as P

F32, BF16 = jnp.float32, jnp.bfloat16
MESH = pl.DeviceIdType.MESH
ORDER = (2, 1, 3, 0)
START = (0, 8, 12, 14)
OFF = (None, 0, 32, 48, 56, 60, 62)


def nt(a, b):
    return lax.dot_general(a, b, (((1,), (1,)), ((), ())), preferred_element_type=F32)


def nn(a, b):
    return lax.dot_general(a, b, (((1,), (0,)), ((), ())), preferred_element_type=F32)


def row_of(level):
    return 3 * START[level] + (8 >> level)


def within(index, size):
    return jnp.minimum(jnp.maximum(index, 0), size - 1)


def low_half(shape):
    return lax.broadcasted_iota(jnp.int32, shape, 1) < 64


def paired(t):
    t = t.astype(F32)
    r = pltpu.roll(t, 64, 1)
    m = low_half(t.shape)
    z = jnp.zeros_like(t)
    top = jnp.concatenate([jnp.where(m, t, z), jnp.where(m, r, z)], axis=1)
    low = jnp.concatenate([jnp.where(m, z, r), jnp.where(m, z, t)], axis=1)
    return jnp.concatenate([top, low], axis=0).astype(BF16)


def split(f):
    hi = f.astype(BF16)
    lo = (f - hi.astype(F32)).astype(BF16)
    return hi, lo


def lowered(f, bd):
    hi, lo = split(f)
    return nn(jnp.concatenate([hi, lo], axis=1), jnp.concatenate([bd, bd], axis=0))


def kernel(
    vectors,
    near_blocks,
    near_cols,
    near_count,
    col_basis,
    row_basis,
    local_transfer,
    local_coupling,
    local_partners,
    upper_transfer,
    upper_coupling,
    upper_partners,
    out,
    wide0,
    wide1,
    wide2,
    wide3,
    nb,
    cb,
    rb,
    lt,
    lc,
    ut,
    ut1,
    ucp,
    ints,
    win,
    field,
    bdt,
    bdu,
    dnh,
    dnl,
    rootpair,
    gbuf,
    ups,
    send_buf,
    recv_buf,
    acc,
    loc_sem,
    own_sem,
    nb_sem,
    anc_sem,
    halo_send,
    halo_recv,
    coef_send,
    coef_recv,
    y_send,
    y_recv,
    i_send,
    i_recv,
    mate_sem,
    x_send,
    x_recv,
    z_send,
    z_recv,
    s_send,
    s_recv,
):
    l = lax.axis_index("leaf")
    y = lax.axis_index("near")
    left = lax.rem(l + 63, 64)
    right = lax.rem(l + 1, 64)
    core = lax.rem(l, 2)
    chip = l // 2
    x = lax.rem(chip, 4)
    z = chip // 4
    mate = l + 1 - 2 * core
    wides = (wide0, wide1, wide2, wide3)
    xs = [(z * 4 + lax.rem(x + d, 4)) * 2 + core for d in range(1, 4)]
    zs = [(lax.rem(z + d, 8) * 4 + x) * 2 + core for d in range(1, 8)]
    ys = [lax.rem(y + d, 4) for d in range(1, 4)]
    rows = [pl.multiple_of(lax.rem(y + d, 4) * 64, 64) for d in ORDER]
    ancestors = [None] + [OFF[m] + l // (1 << m) for m in range(1, 7)]

    def here(src, dst, sem):
        c = pltpu.make_async_copy(src, dst, sem)
        c.start()
        return c

    own = [
        [
            here(
                vectors.at[pl.ds(rows[p], 64), pl.ds(256 * i, 256)],
                wides[p].at[8 + i],
                own_sem.at[p, i],
            )
            for i in range(8)
        ]
        for p in range(4)
    ]
    get_cb = here(col_basis, cb, loc_sem.at[4])
    get_lt = here(local_transfer, lt, loc_sem.at[5])
    get_anc = [
        here(upper_coupling.at[ancestors[m]], ucp.at[0, m - 1], anc_sem.at[m - 1])
        for m in range(1, 7)
    ]
    get_ints = here(upper_partners, ints.at[0], loc_sem.at[6])
    get_ut1 = here(upper_transfer.at[chip], ut1, loc_sem.at[7])
    get_lc = here(local_coupling, lc, loc_sem.at[8])
    get_ut = here(upper_transfer.at[pl.ds(32, 31)], ut, loc_sem.at[9])
    get_rb = here(row_basis, rb, loc_sem.at[10])
    get_nb = [here(near_blocks.at[i], nb.at[i], nb_sem.at[i]) for i in range(8)]

    barrier = pltpu.get_barrier_semaphore()
    for t in [left, right] + xs + zs:
        pl.semaphore_signal(barrier, inc=1, device_id={"leaf": t}, device_id_type=MESH)
    for t in ys:
        pl.semaphore_signal(barrier, inc=1, device_id={"near": t}, device_id_type=MESH)

    get_lt.wait()
    for p in range(7):
        bdt[p] = paired(lt[p])
    for c in get_anc:
        c.wait()
    get_ints.wait()
    pl.semaphore_wait(barrier, 2 + 3 + 7 + 3)

    sends = []

    def remote(src, dst, s, r, target):
        c = pltpu.make_async_remote_copy(
            src_ref=src, dst_ref=dst, send_sem=s, recv_sem=r, device_id=target, device_id_type=MESH
        )
        c.start()
        sends.append(c)
        return c

    def halo(p):
        src = wides[p].at[pl.ds(8, 8)]
        return [
            remote(src, wides[p].at[pl.ds(0, 8)], halo_send.at[p, 0], halo_recv.at[p, 0], {"leaf": right}),
            remote(src, wides[p].at[pl.ds(16, 8)], halo_send.at[p, 1], halo_recv.at[p, 1], {"leaf": left}),
        ]

    for c in own[0]:
        c.wait()
    halos = [halo(0)]
    y_copies = []
    for d in range(1, 4):
        to = {"near": ys[d - 1]}
        y_copies.append(remote(ucp.at[0], ucp.at[d], y_send.at[d - 1], y_recv.at[d - 1], to))
        y_copies.append(remote(upper_partners, ints.at[d], i_send.at[d - 1], i_recv.at[d - 1], to))

    for p in range(1, 4):
        for c in own[p]:
            c.wait()
    get_cb.wait()
    for i in range(8):
        w = cb[:, 256 * i : 256 * (i + 1)]
        none = jnp.zeros_like(w)
        first = jnp.concatenate([wides[p][8 + i, 0:32, :] for p in range(4)], axis=0)
        second = jnp.concatenate([wides[p][8 + i, 32:64, :] for p in range(4)], axis=0)
        f = nt(first, jnp.concatenate([w, none], axis=0)) + nt(second, jnp.concatenate([none, w], axis=0))
        win[row_of(0) + i] = f.astype(BF16)
    for level in range(3):
        for g in range(4 >> level):
            c0 = row_of(level) + 2 * g
            pair = jnp.concatenate([win[c0], win[c0 + 1]], axis=1)
            win[row_of(level + 1) + g] = nt(pair, bdt[START[level + 1] - 8 + g]).astype(BF16)
    rootpair[core] = win[row_of(3), 96:128, :]
    mate_copy = remote(
        rootpair.at[core], rootpair.at[core], mate_sem.at[0], mate_sem.at[1], {"leaf": mate}
    )
    coef_copies = []
    for level in range(4):
        count = 8 >> level
        src = win.at[pl.ds(row_of(level), count)]
        for side, to in ((0, right), (1, left)):
            at = 3 * START[level] + 2 * side * count
            coef_copies.append(
                remote(src, win.at[pl.ds(at, count)], coef_send.at[level, side], coef_recv.at[level, side], {"leaf": to})
            )
    for p in range(1, 4):
        halos.append(halo(p))

    get_ut1.wait()
    bd1 = paired(ut1[...])
    mate_copy.wait_recv()
    gbuf[chip] = nt(jnp.concatenate([rootpair[0], rootpair[1]], axis=1), bd1).astype(BF16)
    x_copies = [
        remote(gbuf.at[chip], gbuf.at[chip], x_send.at[d], x_recv.at[d], {"leaf": xs[d]}) for d in range(3)
    ]

    get_ut.wait()
    for p in range(31):
        bdu[p] = paired(ut[p])

    def near_rows(p, i):
        total = jnp.zeros((64, 256), F32)
        for s in range(8):
            taken = wides[p][within(near_cols[i, s] - (l - 1) * 8, 24)]
            live = jnp.full((64, 256), near_count[i], jnp.int32) > y * 8 + s
            taken = jnp.where(live, taken, jnp.zeros_like(taken))
            total = total + nn(taken, nb[i, s])
        return total

    def far_rows(p, i):
        hi = dnh[i, 32 * p : 32 * p + 32, :].astype(F32)
        lo = dnl[i, 32 * p : 32 * p + 32, :].astype(F32)
        m = low_half((32, 128))
        none = jnp.zeros((32, 128), F32)
        top = jnp.concatenate([jnp.where(m, hi, none), jnp.where(m, lo, none)], axis=1)
        low = jnp.concatenate([jnp.where(m, none, hi), jnp.where(m, none, lo)], axis=1)
        f = jnp.concatenate([top, low], axis=0).astype(BF16)
        w = rb[:, pl.ds(pl.multiple_of(i * 256, 256), 256)]
        return nn(f, jnp.concatenate([w, w, w, w], axis=0))

    def lanes(i):
        return pl.ds(pl.multiple_of(i * 256, 256), 256)

    def local_fields():
        for level in range(4):
            count = 8 >> level
            for g in range(count):
                q = START[level] + g
                got = []
                for t in range(2):
                    w = within(local_partners[t, q] - (l - 1) * count, 3 * count)
                    got.append(win[3 * START[level] + w])
                field[q] = nt(jnp.concatenate(got, axis=1), paired(lc[q]))

    def descend(begin, end, extra):
        top = field[14, begin:end, :]
        downs = [top if extra is None else top + extra]
        for level in (2, 1, 0):
            lower = []
            for g, f in enumerate(downs):
                both = lowered(f, bdt[START[level + 1] - 8 + g])
                q = START[level] + 2 * g
                lower.append(both[:, 0:128] + field[q, begin:end, :])
                lower.append(both[:, 128:256] + field[q + 1, begin:end, :])
            downs = lower
        for i, f in enumerate(downs):
            hi, lo = split(f)
            dnh[i, begin:end, :] = hi
            dnl[i, begin:end, :] = lo

    def chunk(p):
        for c in halos[p]:
            c.wait_recv()
        if p == 0:
            for c in get_nb:
                c.wait()

        def step(i, carry):
            total = near_rows(p, i) + far_rows(p, i)
            if p < 3:
                send_buf[p, :, lanes(i)] = total.astype(BF16)
            else:
                acc[:, lanes(i)] = total
            return carry

        lax.fori_loop(0, 8, step, 0)
        if p < 3:
            d = ORDER[p]
            return remote(
                send_buf.at[p], recv_buf.at[p], s_send.at[p], s_recv.at[p], {"near": ys[d - 1]}
            )

    for c in x_copies:
        c.wait_recv()
    plane = pl.ds(z * 4, 4)
    z_copies = [
        remote(gbuf.at[plane], gbuf.at[plane], z_send.at[d], z_recv.at[d], {"leaf": zs[d]}) for d in range(7)
    ]

    for c in coef_copies:
        c.wait_recv()
    get_lc.wait()
    local_fields()
    descend(0, 96, None)
    get_rb.wait()
    sums = [chunk(0), chunk(1)]

    for c in z_copies:
        c.wait_recv()
    for m in range(2, 7):
        for p in range(64 >> m):
            if m == 2:
                pair = [gbuf[2 * p], gbuf[2 * p + 1]]
            else:
                c0 = OFF[m - 1] - 32 + 2 * p
                pair = [ups[c0], ups[c0 + 1]]
            row = OFF[m] - 32 + p
            ups[row] = nt(jnp.concatenate(pair, axis=1), bdu[row]).astype(BF16)
    for c in y_copies:
        c.wait_recv()
    down = None
    for m in range(6, 0, -1):
        f = None
        for d in range(4):
            got = []
            for t in range(2):
                q = within(ints[d, t, ancestors[m]], 64 >> m)
                got.append(gbuf[q] if m == 1 else ups[OFF[m] - 32 + q])
            part = nt(jnp.concatenate(got, axis=1), paired(ucp[d, m - 1]))
            f = part if f is None else f + part
        if down is not None:
            f = f + down
        both = lowered(f, bd1 if m == 1 else bdu[ancestors[m] - 32])
        even = lax.rem(l // (1 << (m - 1)), 2) == 0
        down = jnp.where(even, both[:, 0:128], both[:, 128:256])
    descend(96, 128, down)

    sums.append(chunk(2))
    chunk(3)
    for c in sums:
        c.wait_recv()
    out[...] = (
        acc[...] + recv_buf[0].astype(F32) + recv_buf[1].astype(F32) + recv_buf[2].astype(F32)
    ).astype(BF16)
    for c in sends:
        c.wait_send()


def local(
    vectors,
    near_blocks,
    near_cols,
    near_count,
    col_basis,
    row_basis,
    local_transfer,
    local_coupling,
    local_partners,
    upper_transfer,
    upper_coupling,
    upper_partners,
):
    anywhere = pl.BlockSpec(memory_space=pl.ANY)
    scalars = pl.BlockSpec(memory_space=pltpu.SMEM)
    dma = pltpu.SemaphoreType.DMA
    vm = pltpu.VMEM
    return pl.pallas_call(
        kernel,
        out_shape=jax.ShapeDtypeStruct((64, 2048), BF16),
        in_specs=[
            anywhere,
            anywhere,
            scalars,
            scalars,
            anywhere,
            anywhere,
            anywhere,
            anywhere,
            scalars,
            anywhere,
            anywhere,
            anywhere,
        ],
        out_specs=pl.BlockSpec(memory_space=pltpu.VMEM),
        scratch_shapes=[vm((24, 64, 256), BF16) for _ in range(4)]
        + [
            vm((8, 8, 256, 256), BF16),
            vm((64, 2048), BF16),
            vm((64, 2048), BF16),
            vm((7, 64, 128), BF16),
            vm((15, 64, 128), BF16),
            vm((31, 64, 128), BF16),
            vm((64, 128), BF16),
            vm((4, 6, 64, 128), BF16),
            pltpu.SMEM((4, 2, 63), jnp.int32),
            vm((45, 128, 128), BF16),
            vm((15, 128, 128), F32),
            vm((7, 128, 256), BF16),
            vm((31, 128, 256), BF16),
            vm((8, 128, 128), BF16),
            vm((8, 128, 128), BF16),
            vm((2, 32, 128), BF16),
            vm((32, 32, 128), BF16),
            vm((31, 32, 128), BF16),
            vm((3, 64, 2048), BF16),
            vm((3, 64, 2048), BF16),
            vm((64, 2048), F32),
            dma((11,)),
            dma((4, 8)),
            dma((8,)),
            dma((6,)),
            dma((4, 2)),
            dma((4, 2)),
            dma((4, 2)),
            dma((4, 2)),
            dma((3,)),
            dma((3,)),
            dma((3,)),
            dma((3,)),
            dma((2,)),
            dma((3,)),
            dma((3,)),
            dma((7,)),
            dma((7,)),
            dma((3,)),
            dma((3,)),
        ],
        compiler_params=pltpu.CompilerParams(
            collective_id=0, has_side_effects=True, vmem_limit_bytes=63 * 1024 * 1024
        ),
        name="h2",
    )(
        vectors,
        near_blocks,
        near_cols,
        near_count,
        col_basis,
        row_basis,
        local_transfer,
        local_coupling,
        local_partners.T,
        upper_transfer,
        upper_coupling,
        upper_partners.T,
    )


def solution(mesh):
    return jax.shard_map(
        local,
        mesh=mesh,
        in_specs=(
            P(None, "leaf"),
            P("leaf", "near", None, None),
            P("leaf", "near"),
            P("leaf"),
            P(None, "leaf"),
            P(None, "leaf"),
            P("leaf", None, None),
            P("leaf", None, "near"),
            P("leaf", "near"),
            P(),
            P(None, None, "near"),
            P(None, "near"),
        ),
        out_specs=P("near", "leaf"),
        check_vma=False,
    )
```

time: 235 us -> 54.2 us (0.23)
  waiting for transfers between devices: 78 us -> 0 us
  local copies, waits for them, and re-layouts: 57.2 us -> 1.67 us
  Pallas kernels: 0 us -> 52.2 us
  matrix products: 33.5 us -> 0 us
  starting transfers between devices: 27.8 us -> 0 us
  other arithmetic: 21.2 us -> 0 us
  between operations: 15.8 us -> 0.01 us
    pallas_call x0 -> x1, Pallas kernels: none -> 52.2 us  [local(): pl.pallas_call(kernel, out_shape=jax.ShapeDtypeStruct((64, 2048), BF16),...]
    all_gather x1 -> x0, waiting for transfers between devices: 42.9 us -> none  [local(): summit = lax.all_gather(coefs[-1], 'leaf', axis=0, tiled=True)]
    dot_general x31 -> x0, matrix products: 33.5 us -> none  [the longest x1 9 us: local(): jnp.einsum('cisa,isab->cib', picked, near_blocks, preferred_element_type=...]
    ppermute x10 -> x0, starting transfers between devices: 27.7 us -> none  [the longest x5 17.8 us: extended(): before = lax.ppermute(last, axis, up)]
    unnamed x29 -> x1, local copies, waits for them, and re-layouts: 27.5 us -> 1.67 us
    ppermute x10 -> x0, waiting for transfers between devices: 17.7 us -> none  [the longest x5 9.18 us: extended(): after = lax.ppermute(initial, axis, down)]
    reduce_scatter x1 -> x0, waiting for transfers between devices: 14.9 us -> none  [local(): lax.psum_scatter(near_terms, 'near', scatter_dimension=0, tiled=True)]
    gather x10 -> x0, local copies, waits for them, and re-layouts: 10.9 us -> none  [the longest x1 5.66 us: local(): jnp.take(wide_leaves, local_cols.reshape(-1), axis=1)]
  transfers between devices with their start and end apart: 14 -> 0, of which waited for: 6 -> 0; matrix products, arithmetic and copies ran while one was open for 44% -> 0% of each run, Pallas kernels for 0% -> 0%
where the time goes in v1:
time: 54.2 us; the launch traced here: 53.8 us
  Pallas kernels  52.2 us (96%)
  local copies, waits for them, and re-layouts  1.67 us (3%)
    pallas_call x1, Pallas kernels, local(): pl.pallas_call(kernel, out_shape=jax.ShapeDtypeStruct((64, 2048), BF16),...  52.2 us
    unnamed x1, local copies, waits for them, and re-layouts  1.67 us

profile of v1, /device:TPU:1, one launch (start us, length us, event | category | flops | bytes accessed | tf_op | source)
XLA Modules:
  0.0 53.8 jit_solution(5383200556934067364)
XLA Ops:
  0.0 52.2 %h2.1 = bf16[64,2048]{1,0:T(8,128)(2,1)} custom-call(bf16[256,2048]{1,0:T(8,128)(2,1)} %vectors.1, bf16[8,8,256,256]{3,2,1,0:T(8,128)(2,1)} %near_blocks.1, s32[8,8]{1,0:T(8,128)} %near_cols.1, s32[8]{0:T(128)} %near_count.1, bf16[64,2048]{1,0:T(8,128)(2,1)} %col_basis.1, bf16[64,2048]{1,0:T(8,128)(2,1)} %row_basis.1, bf16[7,64,128]{2,1,0:T(8,128)(2,1)} %local_transfer.1, ...), custom_call_target="tpu_custom_call" | custom-call | tf_op jit(solution)/shard_map/h2/pallas_call | solution.py:392
  52.2 1.7 %copy.14 = bf16[64,2048]{1,0:T(8,128)(2,1)} copy(bf16[64,2048]{1,0:T(8,128)(2,1)} %h2.1) | data formatting | bytes 524288

commit v2 on v1

--- a/solution.py
+++ b/solution.py
@@ -9,7 +9,7 @@
 
 F32, BF16 = jnp.float32, jnp.bfloat16
 MESH = pl.DeviceIdType.MESH
-ORDER = (2, 1, 3, 0)
+ORDER = (1, 3, 2, 0)
 START = (0, 8, 12, 14)
 OFF = (None, 0, 32, 48, 56, 60, 62)
 
@@ -20,10 +20,6 @@
 
 def nn(a, b):
     return lax.dot_general(a, b, (((1,), (0,)), ((), ())), preferred_element_type=F32)
-
-
-def row_of(level):
-    return 3 * START[level] + (8 >> level)
 
 
 def within(index, size):
@@ -76,6 +72,7 @@
     nb,
     cb,
     rb,
+    rb4,
     lt,
     lc,
     ut,
@@ -86,11 +83,14 @@
     field,
     bdt,
     bdu,
-    dnh,
-    dnl,
+    unfolded,
     rootpair,
     gbuf,
     ups,
+    down_send,
+    downs,
+    hop_send,
+    hop_recv,
     send_buf,
     recv_buf,
     acc,
@@ -106,7 +106,11 @@
     y_recv,
     i_send,
     i_recv,
+    share_send,
+    share_recv,
     mate_sem,
+    down_sem,
+    ucp_sem,
     x_send,
     x_recv,
     z_send,
@@ -116,9 +120,10 @@
 ):
     l = lax.axis_index("leaf")
     y = lax.axis_index("near")
-    left = lax.rem(l + 63, 64)
-    right = lax.rem(l + 1, 64)
     core = lax.rem(l, 2)
+    outer = lax.rem(l + 63 + 2 * core, 64)
+    outer_side = 2 - 2 * core
+    mate_side = 2 * core
     chip = l // 2
     x = lax.rem(chip, 4)
     z = chip // 4
@@ -129,6 +134,12 @@
     ys = [lax.rem(y + d, 4) for d in range(1, 4)]
     rows = [pl.multiple_of(lax.rem(y + d, 4) * 64, 64) for d in ORDER]
     ancestors = [None] + [OFF[m] + l // (1 << m) for m in range(1, 7)]
+
+    barrier = pltpu.get_barrier_semaphore()
+    for t in [outer, mate] + xs + zs:
+        pl.semaphore_signal(barrier, inc=1, device_id={"leaf": t}, device_id_type=MESH)
+    for t in ys:
+        pl.semaphore_signal(barrier, inc=1, device_id={"near": t}, device_id_type=MESH)
 
     def here(src, dst, sem):
         c = pltpu.make_async_copy(src, dst, sem)
@@ -159,20 +170,6 @@
     get_rb = here(row_basis, rb, loc_sem.at[10])
     get_nb = [here(near_blocks.at[i], nb.at[i], nb_sem.at[i]) for i in range(8)]
 
-    barrier = pltpu.get_barrier_semaphore()
-    for t in [left, right] + xs + zs:
-        pl.semaphore_signal(barrier, inc=1, device_id={"leaf": t}, device_id_type=MESH)
-    for t in ys:
-        pl.semaphore_signal(barrier, inc=1, device_id={"near": t}, device_id_type=MESH)
-
-    get_lt.wait()
-    for p in range(7):
-        bdt[p] = paired(lt[p])
-    for c in get_anc:
-        c.wait()
-    get_ints.wait()
-    pl.semaphore_wait(barrier, 2 + 3 + 7 + 3)
-
     sends = []
 
     def remote(src, dst, s, r, target):
@@ -183,23 +180,15 @@
         sends.append(c)
         return c
 
-    def halo(p):
-        src = wides[p].at[pl.ds(8, 8)]
-        return [
-            remote(src, wides[p].at[pl.ds(0, 8)], halo_send.at[p, 0], halo_recv.at[p, 0], {"leaf": right}),
-            remote(src, wides[p].at[pl.ds(16, 8)], halo_send.at[p, 1], halo_recv.at[p, 1], {"leaf": left}),
-        ]
-
-    for c in own[0]:
-        c.wait()
-    halos = [halo(0)]
-    y_copies = []
-    for d in range(1, 4):
-        to = {"near": ys[d - 1]}
-        y_copies.append(remote(ucp.at[0], ucp.at[d], y_send.at[d - 1], y_recv.at[d - 1], to))
-        y_copies.append(remote(upper_partners, ints.at[d], i_send.at[d - 1], i_recv.at[d - 1], to))
-
-    for p in range(1, 4):
+    def halo(p, to, side, k):
+        return remote(
+            wides[p].at[pl.ds(8, 8)], wides[p].at[pl.ds(8 * side, 8)], halo_send.at[p, k], halo_recv.at[p, k], {"leaf": to}
+        )
+
+    get_lt.wait()
+    for p in range(7):
+        bdt[p] = paired(lt[p])
+    for p in range(4):
         for c in own[p]:
             c.wait()
     get_cb.wait()
@@ -209,27 +198,40 @@
         first = jnp.concatenate([wides[p][8 + i, 0:32, :] for p in range(4)], axis=0)
         second = jnp.concatenate([wides[p][8 + i, 32:64, :] for p in range(4)], axis=0)
         f = nt(first, jnp.concatenate([w, none], axis=0)) + nt(second, jnp.concatenate([none, w], axis=0))
-        win[row_of(0) + i] = f.astype(BF16)
+        win[1, i] = f.astype(BF16)
     for level in range(3):
         for g in range(4 >> level):
-            c0 = row_of(level) + 2 * g
-            pair = jnp.concatenate([win[c0], win[c0 + 1]], axis=1)
-            win[row_of(level + 1) + g] = nt(pair, bdt[START[level + 1] - 8 + g]).astype(BF16)
-    rootpair[core] = win[row_of(3), 96:128, :]
+            c0 = START[level] + 2 * g
+            pair = jnp.concatenate([win[1, c0], win[1, c0 + 1]], axis=1)
+            win[1, START[level + 1] + g] = nt(pair, bdt[START[level + 1] - 8 + g]).astype(BF16)
+    mine = pl.ds(pl.multiple_of(96 + 16 * core, 16), 16)
+    other = pl.ds(pl.multiple_of(112 - 16 * core, 16), 16)
+    rootpair[core] = win[1, 14, mine, :]
+    get_rb.wait()
+    for c in get_anc:
+        c.wait()
+    get_ints.wait()
+
+    pl.semaphore_wait(barrier, 2 + 3 + 7 + 3)
     mate_copy = remote(
-        rootpair.at[core], rootpair.at[core], mate_sem.at[0], mate_sem.at[1], {"leaf": mate}
+        win.at[1, 14, other], rootpair.at[core], mate_sem.at[0], mate_sem.at[1], {"leaf": mate}
     )
-    coef_copies = []
-    for level in range(4):
-        count = 8 >> level
-        src = win.at[pl.ds(row_of(level), count)]
-        for side, to in ((0, right), (1, left)):
-            at = 3 * START[level] + 2 * side * count
-            coef_copies.append(
-                remote(src, win.at[pl.ds(at, count)], coef_send.at[level, side], coef_recv.at[level, side], {"leaf": to})
-            )
-    for p in range(1, 4):
-        halos.append(halo(p))
+    y_copies, i_copies = [], []
+    some = pl.ds(3 * core, 3)
+    for d in range(1, 4):
+        to = {"near": ys[d - 1]}
+        y_copies.append(remote(ucp.at[0, some], ucp.at[d, some], y_send.at[d - 1], y_recv.at[d - 1], to))
+        i_copies.append(remote(upper_partners, ints.at[d], i_send.at[d - 1], i_recv.at[d - 1], to))
+    outer_coefs = remote(
+        win.at[1, :, pl.ds(64, 64)],
+        win.at[outer_side, :, pl.ds(64, 64)],
+        coef_send.at[0],
+        coef_recv.at[0],
+        {"leaf": outer},
+    )
+    outer_halos = {2: halo(2, outer, outer_side, 0)}
+    mate_coefs = remote(win.at[1], win.at[mate_side], coef_send.at[1], coef_recv.at[1], {"leaf": mate})
+    mate_halos = [halo(p, mate, mate_side, 1) for p in range(4)]
 
     get_ut1.wait()
     bd1 = paired(ut1[...])
@@ -238,7 +240,23 @@
     x_copies = [
         remote(gbuf.at[chip], gbuf.at[chip], x_send.at[d], x_recv.at[d], {"leaf": xs[d]}) for d in range(3)
     ]
-
+    outer_coefs.wait_recv()
+    got = 2 * core
+    shares = [
+        remote(
+            win.at[got, :, pl.ds(96, 32)],
+            win.at[got, :, pl.ds(32 * p, 32)],
+            share_send.at[p],
+            share_recv.at[p],
+            {"near": ys[3 - ORDER[p]]},
+        )
+        for p in range(2)
+    ]
+    outer_halos[0] = halo(0, outer, outer_side, 0)
+
+    for i in range(8):
+        w = rb[:, 256 * i : 256 * (i + 1)]
+        rb4[i] = jnp.concatenate([w, w, w, w], axis=0)
     get_ut.wait()
     for p in range(31):
         bdu[p] = paired(ut[p])
@@ -253,15 +271,7 @@
         return total
 
     def far_rows(p, i):
-        hi = dnh[i, 32 * p : 32 * p + 32, :].astype(F32)
-        lo = dnl[i, 32 * p : 32 * p + 32, :].astype(F32)
-        m = low_half((32, 128))
-        none = jnp.zeros((32, 128), F32)
-        top = jnp.concatenate([jnp.where(m, hi, none), jnp.where(m, lo, none)], axis=1)
-        low = jnp.concatenate([jnp.where(m, none, hi), jnp.where(m, none, lo)], axis=1)
-        f = jnp.concatenate([top, low], axis=0).astype(BF16)
-        w = rb[:, pl.ds(pl.multiple_of(i * 256, 256), 256)]
-        return nn(f, jnp.concatenate([w, w, w, w], axis=0))
+        return nn(unfolded[p, i], rb4[i])
 
     def lanes(i):
         return pl.ds(pl.multiple_of(i * 256, 256), 256)
@@ -274,7 +284,8 @@
                 got = []
                 for t in range(2):
                     w = within(local_partners[t, q] - (l - 1) * count, 3 * count)
-                    got.append(win[3 * START[level] + w])
+                    side = lax.shift_right_logical(w, 3 - level)
+                    got.append(win[side, START[level] + w - side * count])
                 field[q] = nt(jnp.concatenate(got, axis=1), paired(lc[q]))
 
     def descend(begin, end, extra):
@@ -289,30 +300,39 @@
                 lower.append(both[:, 128:256] + field[q + 1, begin:end, :])
             downs = lower
         for i, f in enumerate(downs):
-            hi, lo = split(f)
-            dnh[i, begin:end, :] = hi
-            dnl[i, begin:end, :] = lo
-
-    def chunk(p):
-        for c in halos[p]:
-            c.wait_recv()
-        if p == 0:
-            for c in get_nb:
-                c.wait()
-
-        def step(i, carry):
-            total = near_rows(p, i) + far_rows(p, i)
-            if p < 3:
-                send_buf[p, :, lanes(i)] = total.astype(BF16)
+            for p in range(begin // 32, end // 32):
+                rows32 = f[32 * p - begin : 32 * p - begin + 32, :]
+                none = jnp.zeros_like(rows32)
+                m = low_half((32, 128))
+                both = jnp.concatenate([jnp.where(m, rows32, none), jnp.where(m, none, rows32)], axis=0)
+                hi, lo = split(both)
+                unfolded[p, i] = jnp.concatenate([hi, lo], axis=1)
+
+    def half(p, h):
+        def step(k, carry):
+            i = 4 * h + k
+            near = acc[:, lanes(i)] if p == 2 else near_rows(p, i)
+            total = near + far_rows(p, i)
+            if (p, h) == (0, 0):
+                total = total + hop_recv[0, :, lanes(k)].astype(F32)
+            if (p, h) == (1, 1):
+                total = total + hop_recv[1, :, lanes(k)].astype(F32)
+            if p == 2:
+                hop_send[h, :, lanes(k)] = total.astype(BF16)
+            elif p < 2:
+                send_buf[p, h, :, lanes(k)] = total.astype(BF16)
             else:
                 acc[:, lanes(i)] = total
             return carry
 
-        lax.fori_loop(0, 8, step, 0)
-        if p < 3:
-            d = ORDER[p]
+        lax.fori_loop(0, 4, step, 0, unroll=2)
+        if p == 2:
+            to = ys[0] if h == 0 else ys[2]
+            return remote(hop_send.at[h], hop_recv.at[h], s_send.at[2, h], s_recv.at[2, h], {"near": to})
+        if p < 2:
+            to = ys[0] if p == 0 else ys[2]
             return remote(
-                send_buf.at[p], recv_buf.at[p], s_send.at[p], s_recv.at[p], {"near": ys[d - 1]}
+                send_buf.at[p, h], recv_buf.at[p, h], s_send.at[p, h], s_recv.at[p, h], {"near": to}
             )
 
     for c in x_copies:
@@ -322,13 +342,44 @@
         remote(gbuf.at[plane], gbuf.at[plane], z_send.at[d], z_recv.at[d], {"leaf": zs[d]}) for d in range(7)
     ]
 
-    for c in coef_copies:
+    for c in y_copies:
+        c.wait_recv()
+    ucp_copy = remote(
+        ucp.at[pl.ds(1, 3), some], ucp.at[pl.ds(1, 3), some], ucp_sem.at[0], ucp_sem.at[1], {"leaf": mate}
+    )
+
+    def arrive(p):
+        outer_halos[p].wait_recv()
+        mate_halos[p].wait_recv()
+
+    arrive(2)
+    outer_halos[1] = halo(1, outer, outer_side, 0)
+    for c in get_nb:
+        c.wait()
+
+    def near_step(i, carry):
+        acc[:, lanes(i)] = near_rows(2, i)
+        return carry
+
+    lax.fori_loop(0, 8, near_step, 0, unroll=2)
+    mate_coefs.wait_recv()
+    for c in shares:
         c.wait_recv()
     get_lc.wait()
     local_fields()
     descend(0, 96, None)
-    get_rb.wait()
-    sums = [chunk(0), chunk(1)]
+    hops = [half(2, 0), half(2, 1)]
+
+    arrive(0)
+    outer_halos[3] = halo(3, outer, outer_side, 0)
+    sums = [half(0, 1)]
+    hops[0].wait_recv()
+    sums.append(half(0, 0))
+
+    arrive(1)
+    sums.append(half(1, 0))
+    hops[1].wait_recv()
+    sums.append(half(1, 1))
 
     for c in z_copies:
         c.wait_recv()
@@ -341,7 +392,8 @@
                 pair = [ups[c0], ups[c0 + 1]]
             row = OFF[m] - 32 + p
             ups[row] = nt(jnp.concatenate(pair, axis=1), bdu[row]).astype(BF16)
-    for c in y_copies:
+    ucp_copy.wait_recv()
+    for c in i_copies:
         c.wait_recv()
     down = None
     for m in range(6, 0, -1):
@@ -358,15 +410,23 @@
         both = lowered(f, bd1 if m == 1 else bdu[ancestors[m] - 32])
         even = lax.rem(l // (1 << (m - 1)), 2) == 0
         down = jnp.where(even, both[:, 0:128], both[:, 128:256])
-    descend(96, 128, down)
-
-    sums.append(chunk(2))
-    chunk(3)
+        if m == 1:
+            down_send[...] = jnp.where(even, both[:, 128:256], both[:, 0:128])
+            downs[core] = down
+    down_copy = remote(down_send, downs.at[core], down_sem.at[0], down_sem.at[1], {"leaf": mate})
+    down_copy.wait_recv()
+    descend(96, 128, jnp.concatenate([downs[0], downs[1]], axis=0))
+
+    arrive(3)
+    half(3, 0)
+    half(3, 1)
     for c in sums:
         c.wait_recv()
-    out[...] = (
-        acc[...] + recv_buf[0].astype(F32) + recv_buf[1].astype(F32) + recv_buf[2].astype(F32)
-    ).astype(BF16)
+    for h in range(2):
+        at = pl.ds(1024 * h, 1024)
+        out[:, at] = (
+            acc[:, at] + recv_buf[0, h].astype(F32) + recv_buf[1, h].astype(F32)
+        ).astype(BF16)
     for c in sends:
         c.wait_send()
 
@@ -412,23 +472,27 @@
             vm((8, 8, 256, 256), BF16),
             vm((64, 2048), BF16),
             vm((64, 2048), BF16),
+            vm((8, 256, 256), BF16),
             vm((7, 64, 128), BF16),
             vm((15, 64, 128), BF16),
             vm((31, 64, 128), BF16),
             vm((64, 128), BF16),
             vm((4, 6, 64, 128), BF16),
             pltpu.SMEM((4, 2, 63), jnp.int32),
-            vm((45, 128, 128), BF16),
+            vm((3, 15, 128, 128), BF16),
             vm((15, 128, 128), F32),
             vm((7, 128, 256), BF16),
             vm((31, 128, 256), BF16),
-            vm((8, 128, 128), BF16),
-            vm((8, 128, 128), BF16),
-            vm((2, 32, 128), BF16),
-            vm((32, 32, 128), BF16),
-            vm((31, 32, 128), BF16),
-            vm((3, 64, 2048), BF16),
-            vm((3, 64, 2048), BF16),
+            vm((4, 8, 64, 256), BF16),
+            vm((2, 16, 128), BF16),
+            vm((32, 16, 128), BF16),
+            vm((31, 16, 128), BF16),
+            vm((16, 128), F32),
+            vm((2, 16, 128), F32),
+            vm((2, 64, 1024), BF16),
+            vm((2, 64, 1024), BF16),
+            vm((2, 2, 64, 1024), BF16),
+            vm((2, 2, 64, 1024), BF16),
             vm((64, 2048), F32),
             dma((11,)),
             dma((4, 8)),
@@ -436,19 +500,23 @@
             dma((6,)),
             dma((4, 2)),
             dma((4, 2)),
-            dma((4, 2)),
-            dma((4, 2)),
+            dma((2,)),
+            dma((2,)),
             dma((3,)),
             dma((3,)),
             dma((3,)),
             dma((3,)),
             dma((2,)),
+            dma((2,)),
+            dma((2,)),
+            dma((2,)),
+            dma((2,)),
             dma((3,)),
             dma((3,)),
             dma((7,)),
             dma((7,)),
-            dma((3,)),
-            dma((3,)),
+            dma((3, 2)),
+            dma((3, 2)),
         ],
         compiler_params=pltpu.CompilerParams(
             collective_id=0, has_side_effects=True, vmem_limit_bytes=63 * 1024 * 1024

time: 54.2 us -> 43.7 us (0.81)
  Pallas kernels: 52.2 us -> 41.8 us
    pallas_call x1, Pallas kernels: 52.2 us -> 41.8 us  [local(): pl.pallas_call(kernel, out_shape=jax.ShapeDtypeStruct((64, 2048), BF16),...]
where the time goes in v2:
time: 43.7 us; the launch traced here: 43.5 us
  Pallas kernels  41.8 us (96%)
  local copies, waits for them, and re-layouts  1.67 us (4%)
    pallas_call x1, Pallas kernels, local(): pl.pallas_call(kernel, out_shape=jax.ShapeDtypeStruct((64, 2048), BF16),...  41.8 us
    unnamed x1, local copies, waits for them, and re-layouts  1.67 us

profile of v2, /device:TPU:1, one launch (start us, length us, event | category | flops | bytes accessed | tf_op | source)
XLA Modules:
  0.0 43.5 jit_solution(6766698334282584403)
XLA Ops:
  0.0 41.8 %h2.1 = bf16[64,2048]{1,0:T(8,128)(2,1)} custom-call(bf16[256,2048]{1,0:T(8,128)(2,1)} %vectors.1, bf16[8,8,256,256]{3,2,1,0:T(8,128)(2,1)} %near_blocks.1, s32[8,8]{1,0:T(8,128)} %near_cols.1, s32[8]{0:T(128)} %near_count.1, bf16[64,2048]{1,0:T(8,128)(2,1)} %col_basis.1, bf16[64,2048]{1,0:T(8,128)(2,1)} %row_basis.1, bf16[7,64,128]{2,1,0:T(8,128)(2,1)} %local_transfer.1, ...), custom_call_target="tpu_custom_call" | custom-call | tf_op jit(solution)/shard_map/h2/pallas_call | solution.py:452
  41.9 1.7 %copy.14 = bf16[64,2048]{1,0:T(8,128)(2,1)} copy(bf16[64,2048]{1,0:T(8,128)(2,1)} %h2.1) | data formatting | bytes 524288

commit v3 on v2

--- a/solution.py
+++ b/solution.py
@@ -229,7 +229,7 @@
         coef_recv.at[0],
         {"leaf": outer},
     )
-    outer_halos = {2: halo(2, outer, outer_side, 0)}
+    outer_halos = {}
     mate_coefs = remote(win.at[1], win.at[mate_side], coef_send.at[1], coef_recv.at[1], {"leaf": mate})
     mate_halos = [halo(p, mate, mate_side, 1) for p in range(4)]
 
@@ -240,6 +240,7 @@
     x_copies = [
         remote(gbuf.at[chip], gbuf.at[chip], x_send.at[d], x_recv.at[d], {"leaf": xs[d]}) for d in range(3)
     ]
+    outer_halos[2] = halo(2, outer, outer_side, 0)
     outer_coefs.wait_recv()
     got = 2 * core
     shares = [
@@ -252,7 +253,6 @@
         )
         for p in range(2)
     ]
-    outer_halos[0] = halo(0, outer, outer_side, 0)
 
     for i in range(8):
         w = rb[:, 256 * i : 256 * (i + 1)]
@@ -261,13 +261,14 @@
     for p in range(31):
         bdu[p] = paired(ut[p])
 
-    def near_rows(p, i):
-        total = jnp.zeros((64, 256), F32)
-        for s in range(8):
-            taken = wides[p][within(near_cols[i, s] - (l - 1) * 8, 24)]
-            live = jnp.full((64, 256), near_count[i], jnp.int32) > y * 8 + s
+    def near_rows(chunks, i):
+        total = jnp.zeros((64 * len(chunks), 256), F32)
+        for t in range(8):
+            j = within(near_cols[i, t] - (l - 1) * 8, 24)
+            taken = jnp.concatenate([wides[p][j] for p in chunks], axis=0)
+            live = jnp.full(taken.shape, near_count[i], jnp.int32) > y * 8 + t
             taken = jnp.where(live, taken, jnp.zeros_like(taken))
-            total = total + nn(taken, nb[i, s])
+            total = total + nn(taken, nb[i, t])
         return total
 
     def far_rows(p, i):
@@ -308,32 +309,41 @@
                 hi, lo = split(both)
                 unfolded[p, i] = jnp.concatenate([hi, lo], axis=1)
 
-    def half(p, h):
+    def first_half(h):
         def step(k, carry):
             i = 4 * h + k
-            near = acc[:, lanes(i)] if p == 2 else near_rows(p, i)
-            total = near + far_rows(p, i)
-            if (p, h) == (0, 0):
-                total = total + hop_recv[0, :, lanes(k)].astype(F32)
-            if (p, h) == (1, 1):
-                total = total + hop_recv[1, :, lanes(k)].astype(F32)
-            if p == 2:
-                hop_send[h, :, lanes(k)] = total.astype(BF16)
-            elif p < 2:
+            hop_send[h, :, lanes(k)] = (acc[:, lanes(i)] + far_rows(2, i)).astype(BF16)
+            return carry
+
+        lax.fori_loop(0, 4, step, 0, unroll=4)
+        to = ys[0] if h == 0 else ys[2]
+        return remote(hop_send.at[h], hop_recv.at[h], s_send.at[2, h], s_recv.at[2, h], {"near": to})
+
+    def middle_half(h):
+        def step(k, carry):
+            i = 4 * h + k
+            near = near_rows((0, 1), i)
+            passed = hop_recv[h, :, lanes(k)].astype(F32)
+            for p in range(2):
+                total = near[64 * p : 64 * p + 64] + far_rows(p, i)
+                if p == h:
+                    total = total + passed
                 send_buf[p, h, :, lanes(k)] = total.astype(BF16)
-            else:
-                acc[:, lanes(i)] = total
             return carry
 
-        lax.fori_loop(0, 4, step, 0, unroll=2)
-        if p == 2:
-            to = ys[0] if h == 0 else ys[2]
-            return remote(hop_send.at[h], hop_recv.at[h], s_send.at[2, h], s_recv.at[2, h], {"near": to})
-        if p < 2:
-            to = ys[0] if p == 0 else ys[2]
-            return remote(
-                send_buf.at[p, h], recv_buf.at[p, h], s_send.at[p, h], s_recv.at[p, h], {"near": to}
-            )
+        lax.fori_loop(0, 4, step, 0, unroll=4)
+        return [
+            remote(send_buf.at[p, h], recv_buf.at[p, h], s_send.at[p, h], s_recv.at[p, h], {"near": ys[2 * p]})
+            for p in range(2)
+        ]
+
+    def last_half(h):
+        def step(k, carry):
+            i = 4 * h + k
+            acc[:, lanes(i)] = near_rows((3,), i) + far_rows(3, i)
+            return carry
+
+        lax.fori_loop(0, 4, step, 0, unroll=4)
 
     for c in x_copies:
         c.wait_recv()
@@ -342,6 +352,8 @@
         remote(gbuf.at[plane], gbuf.at[plane], z_send.at[d], z_recv.at[d], {"leaf": zs[d]}) for d in range(7)
     ]
 
+    outer_halos[0] = halo(0, outer, outer_side, 0)
+
     for c in y_copies:
         c.wait_recv()
     ucp_copy = remote(
@@ -358,28 +370,20 @@
         c.wait()
 
     def near_step(i, carry):
-        acc[:, lanes(i)] = near_rows(2, i)
+        acc[:, lanes(i)] = near_rows((2,), i)
         return carry
 
-    lax.fori_loop(0, 8, near_step, 0, unroll=2)
+    lax.fori_loop(0, 8, near_step, 0, unroll=4)
     mate_coefs.wait_recv()
     for c in shares:
         c.wait_recv()
     get_lc.wait()
     local_fields()
     descend(0, 96, None)
-    hops = [half(2, 0), half(2, 1)]
+    hops = [first_half(0), first_half(1)]
 
     arrive(0)
     outer_halos[3] = halo(3, outer, outer_side, 0)
-    sums = [half(0, 1)]
-    hops[0].wait_recv()
-    sums.append(half(0, 0))
-
-    arrive(1)
-    sums.append(half(1, 0))
-    hops[1].wait_recv()
-    sums.append(half(1, 1))
 
     for c in z_copies:
         c.wait_recv()
@@ -414,12 +418,19 @@
             down_send[...] = jnp.where(even, both[:, 128:256], both[:, 0:128])
             downs[core] = down
     down_copy = remote(down_send, downs.at[core], down_sem.at[0], down_sem.at[1], {"leaf": mate})
+
+
+    arrive(1)
+    hops[0].wait_recv()
+    sums = middle_half(0)
+    hops[1].wait_recv()
+    sums += middle_half(1)
+
     down_copy.wait_recv()
     descend(96, 128, jnp.concatenate([downs[0], downs[1]], axis=0))
-
     arrive(3)
-    half(3, 0)
-    half(3, 1)
+    last_half(0)
+    last_half(1)
     for c in sums:
         c.wait_recv()
     for h in range(2):

time: 43.7 us -> 38.8 us (0.89)
  the two profiles are of different devices: /device:TPU:1 before, /device:TPU:8 now
where the time goes in v3:
time: 38.8 us; the launch traced here: 38.7 us
  Pallas kernels  37 us (95%)
  local copies, waits for them, and re-layouts  1.67 us (4%)
    pallas_call x1, Pallas kernels, local(): pl.pallas_call(kernel, out_shape=jax.ShapeDtypeStruct((64, 2048), BF16),...  37 us
    unnamed x1, local copies, waits for them, and re-layouts  1.67 us

profile of v3, /device:TPU:8, one launch (start us, length us, event | category | flops | bytes accessed | tf_op | source)
XLA Modules:
  0.0 38.7 jit_solution(6775489431536000056)
XLA Ops:
  0.0 37.0 %h2.1 = bf16[64,2048]{1,0:T(8,128)(2,1)} custom-call(bf16[256,2048]{1,0:T(8,128)(2,1)} %vectors.1, bf16[8,8,256,256]{3,2,1,0:T(8,128)(2,1)} %near_blocks.1, s32[8,8]{1,0:T(8,128)} %near_cols.1, s32[8]{0:T(128)} %near_count.1, bf16[64,2048]{1,0:T(8,128)(2,1)} %col_basis.1, bf16[64,2048]{1,0:T(8,128)(2,1)} %row_basis.1, bf16[7,64,128]{2,1,0:T(8,128)(2,1)} %local_transfer.1, ...), custom_call_target="tpu_custom_call" | custom-call | tf_op jit(solution)/shard_map/h2/pallas_call | solution.py:463
  37.0 1.7 %copy.14 = bf16[64,2048]{1,0:T(8,128)(2,1)} copy(bf16[64,2048]{1,0:T(8,128)(2,1)} %h2.1) | data formatting | bytes 524288

commit v4 on v3

--- a/solution.py
+++ b/solution.py
@@ -94,6 +94,7 @@
     send_buf,
     recv_buf,
     acc,
+    held,
     loc_sem,
     own_sem,
     nb_sem,
@@ -124,6 +125,7 @@
     outer = lax.rem(l + 63 + 2 * core, 64)
     outer_side = 2 - 2 * core
     mate_side = 2 * core
+    inside = jnp.logical_and(l > 0, l < 63)
     chip = l // 2
     x = lax.rem(chip, 4)
     z = chip // 4
@@ -146,6 +148,8 @@
         c.start()
         return c
 
+    get_cb = here(col_basis, cb, loc_sem.at[4])
+    get_lt = here(local_transfer, lt, loc_sem.at[5])
     own = [
         [
             here(
@@ -157,18 +161,12 @@
         ]
         for p in range(4)
     ]
-    get_cb = here(col_basis, cb, loc_sem.at[4])
-    get_lt = here(local_transfer, lt, loc_sem.at[5])
     get_anc = [
         here(upper_coupling.at[ancestors[m]], ucp.at[0, m - 1], anc_sem.at[m - 1])
         for m in range(1, 7)
     ]
     get_ints = here(upper_partners, ints.at[0], loc_sem.at[6])
     get_ut1 = here(upper_transfer.at[chip], ut1, loc_sem.at[7])
-    get_lc = here(local_coupling, lc, loc_sem.at[8])
-    get_ut = here(upper_transfer.at[pl.ds(32, 31)], ut, loc_sem.at[9])
-    get_rb = here(row_basis, rb, loc_sem.at[10])
-    get_nb = [here(near_blocks.at[i], nb.at[i], nb_sem.at[i]) for i in range(8)]
 
     sends = []
 
@@ -179,6 +177,25 @@
         c.start()
         sends.append(c)
         return c
+
+    class Outer:
+        def __init__(self, *args):
+            src, dst, s, r = args
+            self.copy = pltpu.make_async_remote_copy(
+                src_ref=src, dst_ref=dst, send_sem=s, recv_sem=r, device_id={"leaf": outer}, device_id_type=MESH
+            )
+            pl.when(inside)(self.copy.start)
+            sends.append(self)
+
+        def wait_recv(self):
+            pl.when(inside)(self.copy.wait_recv)
+
+        def wait_send(self):
+            pl.when(inside)(self.copy.wait_send)
+
+    def outer_halo(p):
+        src = wides[p].at[pl.ds(8, 8)]
+        return Outer(src, wides[p].at[pl.ds(8 * outer_side, 8)], halo_send.at[p, 0], halo_recv.at[p, 0])
 
     def halo(p, to, side, k):
         return remote(
@@ -204,10 +221,13 @@
             c0 = START[level] + 2 * g
             pair = jnp.concatenate([win[1, c0], win[1, c0 + 1]], axis=1)
             win[1, START[level + 1] + g] = nt(pair, bdt[START[level + 1] - 8 + g]).astype(BF16)
+    get_lc = here(local_coupling, lc, loc_sem.at[8])
+    get_ut = here(upper_transfer.at[pl.ds(32, 31)], ut, loc_sem.at[9])
+    get_rb = here(row_basis, rb, loc_sem.at[10])
+    get_nb = [here(near_blocks.at[i], nb.at[i], nb_sem.at[i]) for i in range(8)]
     mine = pl.ds(pl.multiple_of(96 + 16 * core, 16), 16)
     other = pl.ds(pl.multiple_of(112 - 16 * core, 16), 16)
     rootpair[core] = win[1, 14, mine, :]
-    get_rb.wait()
     for c in get_anc:
         c.wait()
     get_ints.wait()
@@ -215,6 +235,9 @@
     pl.semaphore_wait(barrier, 2 + 3 + 7 + 3)
     mate_copy = remote(
         win.at[1, 14, other], rootpair.at[core], mate_sem.at[0], mate_sem.at[1], {"leaf": mate}
+    )
+    outer_coefs = Outer(
+        win.at[1, :, pl.ds(64, 64)], win.at[outer_side, :, pl.ds(64, 64)], coef_send.at[0], coef_recv.at[0]
     )
     y_copies, i_copies = [], []
     some = pl.ds(3 * core, 3)
@@ -222,13 +245,6 @@
         to = {"near": ys[d - 1]}
         y_copies.append(remote(ucp.at[0, some], ucp.at[d, some], y_send.at[d - 1], y_recv.at[d - 1], to))
         i_copies.append(remote(upper_partners, ints.at[d], i_send.at[d - 1], i_recv.at[d - 1], to))
-    outer_coefs = remote(
-        win.at[1, :, pl.ds(64, 64)],
-        win.at[outer_side, :, pl.ds(64, 64)],
-        coef_send.at[0],
-        coef_recv.at[0],
-        {"leaf": outer},
-    )
     outer_halos = {}
     mate_coefs = remote(win.at[1], win.at[mate_side], coef_send.at[1], coef_recv.at[1], {"leaf": mate})
     mate_halos = [halo(p, mate, mate_side, 1) for p in range(4)]
@@ -236,11 +252,11 @@
     get_ut1.wait()
     bd1 = paired(ut1[...])
     mate_copy.wait_recv()
-    gbuf[chip] = nt(jnp.concatenate([rootpair[0], rootpair[1]], axis=1), bd1).astype(BF16)
-    x_copies = [
-        remote(gbuf.at[chip], gbuf.at[chip], x_send.at[d], x_recv.at[d], {"leaf": xs[d]}) for d in range(3)
+    gbuf[x, z] = nt(jnp.concatenate([rootpair[0], rootpair[1]], axis=1), bd1).astype(BF16)
+    z_copies = [
+        remote(gbuf.at[x, z], gbuf.at[x, z], z_send.at[d], z_recv.at[d], {"leaf": zs[d]}) for d in range(7)
     ]
-    outer_halos[2] = halo(2, outer, outer_side, 0)
+    outer_halos[2] = outer_halo(2)
     outer_coefs.wait_recv()
     got = 2 * core
     shares = [
@@ -254,6 +270,7 @@
         for p in range(2)
     ]
 
+    get_rb.wait()
     for i in range(8):
         w = rb[:, 256 * i : 256 * (i + 1)]
         rb4[i] = jnp.concatenate([w, w, w, w], axis=0)
@@ -319,61 +336,48 @@
         to = ys[0] if h == 0 else ys[2]
         return remote(hop_send.at[h], hop_recv.at[h], s_send.at[2, h], s_recv.at[2, h], {"near": to})
 
-    def middle_half(h):
+    def middle(p, h, near, passed):
         def step(k, carry):
             i = 4 * h + k
-            near = near_rows((0, 1), i)
-            passed = hop_recv[h, :, lanes(k)].astype(F32)
-            for p in range(2):
-                total = near[64 * p : 64 * p + 64] + far_rows(p, i)
-                if p == h:
-                    total = total + passed
-                send_buf[p, h, :, lanes(k)] = total.astype(BF16)
+            total = (near_rows((p,), i) if near else held[:, lanes(k)]) + far_rows(p, i)
+            if passed:
+                total = total + hop_recv[h, :, lanes(k)].astype(F32)
+            send_buf[p, h, :, lanes(k)] = total.astype(BF16)
             return carry
 
         lax.fori_loop(0, 4, step, 0, unroll=4)
-        return [
-            remote(send_buf.at[p, h], recv_buf.at[p, h], s_send.at[p, h], s_recv.at[p, h], {"near": ys[2 * p]})
-            for p in range(2)
-        ]
-
-    def last_half(h):
-        def step(k, carry):
-            i = 4 * h + k
-            acc[:, lanes(i)] = near_rows((3,), i) + far_rows(3, i)
-            return carry
-
-        lax.fori_loop(0, 4, step, 0, unroll=4)
-
-    for c in x_copies:
+        return remote(
+            send_buf.at[p, h], recv_buf.at[p, h], s_send.at[p, h], s_recv.at[p, h], {"near": ys[2 * p]}
+        )
+
+    for c in z_copies:
         c.wait_recv()
-    plane = pl.ds(z * 4, 4)
-    z_copies = [
-        remote(gbuf.at[plane], gbuf.at[plane], z_send.at[d], z_recv.at[d], {"leaf": zs[d]}) for d in range(7)
+    x_copies = [
+        remote(gbuf.at[x], gbuf.at[x], x_send.at[d], x_recv.at[d], {"leaf": xs[d]}) for d in range(3)
     ]
 
-    outer_halos[0] = halo(0, outer, outer_side, 0)
-
+    outer_halos[0] = outer_halo(0)
+
+    def arrive(p):
+        outer_halos[p].wait_recv()
+        mate_halos[p].wait_recv()
+
+    arrive(2)
+    outer_halos[1] = outer_halo(1)
+    for c in get_nb:
+        c.wait()
+
+    def near_step(i, carry):
+        acc[:, lanes(i)] = near_rows((2,), i)
+        return carry
+
+    lax.fori_loop(0, 8, near_step, 0, unroll=4)
     for c in y_copies:
         c.wait_recv()
     ucp_copy = remote(
         ucp.at[pl.ds(1, 3), some], ucp.at[pl.ds(1, 3), some], ucp_sem.at[0], ucp_sem.at[1], {"leaf": mate}
     )
 
-    def arrive(p):
-        outer_halos[p].wait_recv()
-        mate_halos[p].wait_recv()
-
-    arrive(2)
-    outer_halos[1] = halo(1, outer, outer_side, 0)
-    for c in get_nb:
-        c.wait()
-
-    def near_step(i, carry):
-        acc[:, lanes(i)] = near_rows((2,), i)
-        return carry
-
-    lax.fori_loop(0, 8, near_step, 0, unroll=4)
     mate_coefs.wait_recv()
     for c in shares:
         c.wait_recv()
@@ -383,14 +387,28 @@
     hops = [first_half(0), first_half(1)]
 
     arrive(0)
-    outer_halos[3] = halo(3, outer, outer_side, 0)
-
-    for c in z_copies:
+    outer_halos[3] = outer_halo(3)
+
+    sums = [middle(0, 1, True, False)]
+
+    def held_step(k, carry):
+        held[:, lanes(k)] = near_rows((0,), k)
+        return carry
+
+    lax.fori_loop(0, 4, held_step, 0, unroll=4)
+    arrive(1)
+    sums.append(middle(1, 0, True, False))
+    hops[0].wait_recv()
+    sums.append(middle(0, 0, False, True))
+    hops[1].wait_recv()
+    sums.append(middle(1, 1, True, True))
+
+    for c in x_copies:
         c.wait_recv()
     for m in range(2, 7):
         for p in range(64 >> m):
             if m == 2:
-                pair = [gbuf[2 * p], gbuf[2 * p + 1]]
+                pair = [gbuf[2 * p % 4, p // 2], gbuf[2 * p % 4 + 1, p // 2]]
             else:
                 c0 = OFF[m - 1] - 32 + 2 * p
                 pair = [ups[c0], ups[c0 + 1]]
@@ -406,7 +424,10 @@
             got = []
             for t in range(2):
                 q = within(ints[d, t, ancestors[m]], 64 >> m)
-                got.append(gbuf[q] if m == 1 else ups[OFF[m] - 32 + q])
+                if m == 1:
+                    got.append(gbuf[lax.bitwise_and(q, 3), lax.shift_right_logical(q, 2)])
+                else:
+                    got.append(ups[OFF[m] - 32 + q])
             part = nt(jnp.concatenate(got, axis=1), paired(ucp[d, m - 1]))
             f = part if f is None else f + part
         if down is not None:
@@ -420,24 +441,27 @@
     down_copy = remote(down_send, downs.at[core], down_sem.at[0], down_sem.at[1], {"leaf": mate})
 
 
-    arrive(1)
-    hops[0].wait_recv()
-    sums = middle_half(0)
-    hops[1].wait_recv()
-    sums += middle_half(1)
-
+    arrive(3)
+
+    def own_step(i, carry):
+        acc[:, lanes(i)] = near_rows((3,), i)
+        return carry
+
+    lax.fori_loop(0, 8, own_step, 0, unroll=4)
     down_copy.wait_recv()
     descend(96, 128, jnp.concatenate([downs[0], downs[1]], axis=0))
-    arrive(3)
-    last_half(0)
-    last_half(1)
     for c in sums:
         c.wait_recv()
     for h in range(2):
-        at = pl.ds(1024 * h, 1024)
-        out[:, at] = (
-            acc[:, at] + recv_buf[0, h].astype(F32) + recv_buf[1, h].astype(F32)
-        ).astype(BF16)
+
+        def final_step(k, carry):
+            i = 4 * h + k
+            total = acc[:, lanes(i)] + far_rows(3, i)
+            total = total + recv_buf[0, h, :, lanes(k)].astype(F32) + recv_buf[1, h, :, lanes(k)].astype(F32)
+            out[:, lanes(i)] = total.astype(BF16)
+            return carry
+
+        lax.fori_loop(0, 4, final_step, 0, unroll=4)
     for c in sends:
         c.wait_send()
 
@@ -496,7 +520,7 @@
             vm((31, 128, 256), BF16),
             vm((4, 8, 64, 256), BF16),
             vm((2, 16, 128), BF16),
-            vm((32, 16, 128), BF16),
+            vm((4, 8, 16, 128), BF16),
             vm((31, 16, 128), BF16),
             vm((16, 128), F32),
             vm((2, 16, 128), F32),
@@ -505,6 +529,7 @@
             vm((2, 2, 64, 1024), BF16),
             vm((2, 2, 64, 1024), BF16),
             vm((64, 2048), F32),
+            vm((64, 1024), F32),
             dma((11,)),
             dma((4, 8)),
             dma((8,)),

time: 38.8 us -> 36.8 us (0.948)
  the two profiles are of different devices: /device:TPU:8 before, /device:TPU:1 now
where the time goes in v4:
time: 36.8 us; the launch traced here: 36.6 us
  Pallas kernels  34.9 us (95%)
  local copies, waits for them, and re-layouts  1.67 us (5%)
    pallas_call x1, Pallas kernels, local(): pl.pallas_call(kernel, out_shape=jax.ShapeDtypeStruct((64, 2048), BF16),...  34.9 us
    unnamed x1, local copies, waits for them, and re-layouts  1.67 us

profile of v4, /device:TPU:1, one launch (start us, length us, event | category | flops | bytes accessed | tf_op | source)
XLA Modules:
  0.0 36.6 jit_solution(15440659043724450128)
XLA Ops:
  0.0 34.9 %h2.1 = bf16[64,2048]{1,0:T(8,128)(2,1)} custom-call(bf16[256,2048]{1,0:T(8,128)(2,1)} %vectors.1, bf16[8,8,256,256]{3,2,1,0:T(8,128)(2,1)} %near_blocks.1, s32[8,8]{1,0:T(8,128)} %near_cols.1, s32[8]{0:T(128)} %near_count.1, bf16[64,2048]{1,0:T(8,128)(2,1)} %col_basis.1, bf16[64,2048]{1,0:T(8,128)(2,1)} %row_basis.1, bf16[7,64,128]{2,1,0:T(8,128)(2,1)} %local_transfer.1, ...), custom_call_target="tpu_custom_call" | custom-call | tf_op jit(solution)/shard_map/h2/pallas_call | solution.py:487
  34.9 1.7 %copy.14 = bf16[64,2048]{1,0:T(8,128)(2,1)} copy(bf16[64,2048]{1,0:T(8,128)(2,1)} %h2.1) | data formatting | bytes 524288

commit v5 on v4

--- a/solution.py
+++ b/solution.py
@@ -138,7 +138,7 @@
     ancestors = [None] + [OFF[m] + l // (1 << m) for m in range(1, 7)]
 
     barrier = pltpu.get_barrier_semaphore()
-    for t in [outer, mate] + xs + zs:
+    for t in zs + xs + [outer, mate]:
         pl.semaphore_signal(barrier, inc=1, device_id={"leaf": t}, device_id_type=MESH)
     for t in ys:
         pl.semaphore_signal(barrier, inc=1, device_id={"near": t}, device_id_type=MESH)
@@ -236,15 +236,12 @@
     mate_copy = remote(
         win.at[1, 14, other], rootpair.at[core], mate_sem.at[0], mate_sem.at[1], {"leaf": mate}
     )
-    outer_coefs = Outer(
-        win.at[1, :, pl.ds(64, 64)], win.at[outer_side, :, pl.ds(64, 64)], coef_send.at[0], coef_recv.at[0]
-    )
-    y_copies, i_copies = [], []
-    some = pl.ds(3 * core, 3)
-    for d in range(1, 4):
-        to = {"near": ys[d - 1]}
-        y_copies.append(remote(ucp.at[0, some], ucp.at[d, some], y_send.at[d - 1], y_recv.at[d - 1], to))
-        i_copies.append(remote(upper_partners, ints.at[d], i_send.at[d - 1], i_recv.at[d - 1], to))
+    outer_coefs = [
+        Outer(
+            win.at[1, :, pl.ds(begin, 32)], win.at[outer_side, :, pl.ds(begin, 32)], coef_send.at[k], coef_recv.at[k]
+        )
+        for k, begin in ((0, 96), (2, 64))
+    ]
     outer_halos = {}
     mate_coefs = remote(win.at[1], win.at[mate_side], coef_send.at[1], coef_recv.at[1], {"leaf": mate})
     mate_halos = [halo(p, mate, mate_side, 1) for p in range(4)]
@@ -257,7 +254,8 @@
         remote(gbuf.at[x, z], gbuf.at[x, z], z_send.at[d], z_recv.at[d], {"leaf": zs[d]}) for d in range(7)
     ]
     outer_halos[2] = outer_halo(2)
-    outer_coefs.wait_recv()
+    outer_halos[0] = outer_halo(0)
+    outer_coefs[0].wait_recv()
     got = 2 * core
     shares = [
         remote(
@@ -270,6 +268,12 @@
         for p in range(2)
     ]
 
+    y_copies, i_copies = [], []
+    some = pl.ds(3 * core, 3)
+    for d in range(1, 4):
+        to = {"near": ys[d - 1]}
+        y_copies.append(remote(ucp.at[0, some], ucp.at[d, some], y_send.at[d - 1], y_recv.at[d - 1], to))
+        i_copies.append(remote(upper_partners, ints.at[d], i_send.at[d - 1], i_recv.at[d - 1], to))
     get_rb.wait()
     for i in range(8):
         w = rb[:, 256 * i : 256 * (i + 1)]
@@ -350,41 +354,41 @@
             send_buf.at[p, h], recv_buf.at[p, h], s_send.at[p, h], s_recv.at[p, h], {"near": ys[2 * p]}
         )
 
+
+    def arrive(p):
+        outer_halos[p].wait_recv()
+        mate_halos[p].wait_recv()
+
+    arrive(2)
+    outer_halos[1] = outer_halo(1)
+    for c in get_nb:
+        c.wait()
+
+    def near_step(i, carry):
+        acc[:, lanes(i)] = near_rows((2,), i)
+        return carry
+
+    lax.fori_loop(0, 8, near_step, 0, unroll=4)
     for c in z_copies:
         c.wait_recv()
     x_copies = [
         remote(gbuf.at[x], gbuf.at[x], x_send.at[d], x_recv.at[d], {"leaf": xs[d]}) for d in range(3)
     ]
 
-    outer_halos[0] = outer_halo(0)
-
-    def arrive(p):
-        outer_halos[p].wait_recv()
-        mate_halos[p].wait_recv()
-
-    arrive(2)
-    outer_halos[1] = outer_halo(1)
-    for c in get_nb:
-        c.wait()
-
-    def near_step(i, carry):
-        acc[:, lanes(i)] = near_rows((2,), i)
-        return carry
-
-    lax.fori_loop(0, 8, near_step, 0, unroll=4)
-    for c in y_copies:
-        c.wait_recv()
-    ucp_copy = remote(
-        ucp.at[pl.ds(1, 3), some], ucp.at[pl.ds(1, 3), some], ucp_sem.at[0], ucp_sem.at[1], {"leaf": mate}
-    )
-
     mate_coefs.wait_recv()
+    outer_coefs[1].wait_recv()
     for c in shares:
         c.wait_recv()
     get_lc.wait()
     local_fields()
     descend(0, 96, None)
     hops = [first_half(0), first_half(1)]
+    for c in y_copies:
+        c.wait_recv()
+    ucp_copy = remote(
+        ucp.at[pl.ds(1, 3), some], ucp.at[pl.ds(1, 3), some], ucp_sem.at[0], ucp_sem.at[1], {"leaf": mate}
+    )
+
 
     arrive(0)
     outer_halos[3] = outer_halo(3)
@@ -536,8 +540,8 @@
             dma((6,)),
             dma((4, 2)),
             dma((4, 2)),
-            dma((2,)),
-            dma((2,)),
+            dma((3,)),
+            dma((3,)),
             dma((3,)),
             dma((3,)),
             dma((3,)),

time: 36.8 us -> 36.4 us (0.989)
  the two profiles are of different devices: /device:TPU:1 before, /device:TPU:32 now
where the time goes in v5:
time: 36.4 us; the launch traced here: 36.3 us
  Pallas kernels  34.6 us (95%)
  local copies, waits for them, and re-layouts  1.67 us (5%)
    pallas_call x1, Pallas kernels, local(): pl.pallas_call(kernel, out_shape=jax.ShapeDtypeStruct((64, 2048), BF16),...  34.6 us
    unnamed x1, local copies, waits for them, and re-layouts  1.67 us

profile of v5, /device:TPU:32, one launch (start us, length us, event | category | flops | bytes accessed | tf_op | source)
XLA Modules:
  0.0 36.3 jit_solution(2815138856237137825)
XLA Ops:
  0.0 34.6 %h2.1 = bf16[64,2048]{1,0:T(8,128)(2,1)} custom-call(bf16[256,2048]{1,0:T(8,128)(2,1)} %vectors.1, bf16[8,8,256,256]{3,2,1,0:T(8,128)(2,1)} %near_blocks.1, s32[8,8]{1,0:T(8,128)} %near_cols.1, s32[8]{0:T(128)} %near_count.1, bf16[64,2048]{1,0:T(8,128)(2,1)} %col_basis.1, bf16[64,2048]{1,0:T(8,128)(2,1)} %row_basis.1, bf16[7,64,128]{2,1,0:T(8,128)(2,1)} %local_transfer.1, ...), custom_call_target="tpu_custom_call" | custom-call | tf_op jit(solution)/shard_map/h2/pallas_call | solution.py:491
  34.6 1.7 %copy.14 = bf16[64,2048]{1,0:T(8,128)(2,1)} copy(bf16[64,2048]{1,0:T(8,128)(2,1)} %h2.1) | data formatting | bytes 524288
